TPU v7x, 256 devices: a whole 4x4x8 slice. The times are simulated.
256 devices in a mesh: dp: 16 (over z, y_lo), mp: 16 (over x, y_hi, core).
Axes of the slice: x: 4, y: 4 (y_hi: 2, y_lo: 2; y = y_hi * 2 + y_lo), z: 8, core: 2. Of those that a mesh axis runs over, the one named last changes fastest.
Arguments:
- pre_act: bfloat16 [2048, 36864], P('dp', 'mp'), may hold values from -6 to 6
- grad_out: bfloat16 [2048, 18432], P('dp', 'mp'), may hold values from -6 to 6
- row_state: float32 [16, 1152], P(None, 'dp'), may hold values from 3e-05 to 0.0003
- col_state: float32 [36864], P('mp'), may hold values from 3e-05 to 0.0003
Outputs:
- update: bfloat16 [16, 1152, 36864], P(None, 'dp', 'mp')
- row_new: float32 [16, 1152], P(None, 'dp')
- col_new: float32 [36864], P('mp')
All inputs are finite; a program needn't handle non-finite values.
Results may differ from a plain program's by a relative error of at most 0.0015.
The roundings to bfloat16 on the way count: a program that leaves them out, or rounds other values in their place, can miss the bound.
Values may be sent and summed in bfloat16 or wider, within the bound.
No kernel may reach another device: no remote copies, remote signals or barrier semaphores. Data moves between devices by JAX's collectives and lax.ppermute only.
A program may use at most 128 MiB of HBM per device.

v0:
```python
import jax
import jax.numpy as jnp
from jax import lax
from jax.sharding import PartitionSpec as P

D = 18432


decay = 1.0 - 2.0 ** (-0.8)
tiny = 1e-30


def body(pre_act, grad_out, row_state, col_state):
    dp_count = lax.axis_size("dp")
    mp_count = lax.axis_size("mp")
    tok_rows = pre_act.shape[0]
    hid_cols = pre_act.shape[1]
    all_tokens = tok_rows * dp_count
    all_hidden = hid_cols * mp_count
    slice_width = row_state.shape[1]
    own_width = mp_count * slice_width
    hidden = jax.nn.gelu(pre_act.astype(jnp.float32)).astype(jnp.bfloat16)
    full_out = lax.all_gather(grad_out, "mp", axis=1, tiled=True)
    split_out = full_out.reshape(tok_rows, mp_count, dp_count, slice_width)
    moved = lax.all_to_all(split_out, "dp", split_axis=2, concat_axis=0, tiled=True)
    own_cols = moved.reshape(all_tokens, own_width)
    product = lax.dot_general(
        own_cols,
        lax.all_gather(hidden, "dp", axis=0, tiled=True),
        (((0,), (0,)), ((), ())),
        preferred_element_type=jnp.float32,
    )
    grad = product / all_tokens
    squares = grad * grad
    row_flat = row_state.reshape(own_width)
    row_sum = lax.psum(jnp.sum(squares, axis=1), "mp")
    col_sum = lax.psum(jnp.sum(squares, axis=0), "dp")
    row_new = decay * row_flat + (1.0 - decay) * (row_sum / all_hidden + tiny)
    col_new = decay * col_state + (1.0 - decay) * (col_sum / D + tiny)
    scale = lax.psum(jnp.sum(row_new), "dp") / D
    update = (grad * lax.rsqrt(row_new[:, None] * col_new[None, :] / scale)).astype(jnp.bfloat16)
    return (
        update.reshape(mp_count, slice_width, hid_cols),
        row_new.reshape(mp_count, slice_width),
        col_new,
    )


def solution(mesh):
    return jax.shard_map(
        body,
        mesh=mesh,
        in_specs=(P("dp", "mp"), P("dp", "mp"), P(None, "dp"), P("mp")),
        out_specs=(P(None, "dp", "mp"), P(None, "dp"), P("mp")),
        check_vma=False,
    )
```

profile of v0, /device:TPU:0, one launch (start us, length us, event | category | flops | bytes accessed | tf_op | source)
XLA Modules:
  0.0 487.1 jit_solution(11499572299897379973)
XLA Ops:
  7.2 0.0 all-gather.5.cloned.1.call-start
  7.2 1.8 copy.9
  9.1 0.0 all-gather.5.cloned.1.call-update
  9.1 0.0 all-gather.3.cloned.1.call-start
  9.1 2.3 fusion.8
  11.4 0.0 all-gather.3.cloned.1.call-update
  11.5 64.1 %all-gather.5.cloned.1.call-done = bf16[128,18432]{0,1:T(8,128)(2,1)} async-done(((bf16[128,1152]{0,1:T(8,128)(2,1)}), bf16[128,18432]{0,1:T(8,128)(2,1)}) %all-gather.5.cloned.1.call-update) | async-done | bytes 4718608 | tf_op jit(solution)/shard_map/all_gather | solution.py:23
  75.6 5.7 %copy.10 = bf16[128,16,16,72]{0,3,1,2:T(8,128)(2,1)} copy(bf16[128,16,16,72]{0,3,2,1:T(8,128)(2,1)} %bitcast.18) | data formatting | bytes 9437184 | tf_op jit(solution)/shard_map/reshape | solution.py:24
  81.3 0.0 copy-start.2
  81.3 7.3 %all-to-all-start = ((bf16[128,16,16,72]{0,3,1,2:T(8,128)(2,1)}), bf16[128,16,16,72]{0,3,1,2:T(8,128)(2,1)}, u32[]{:S(2)}, u32[]{:S(2)}) async-start(bf16[128,16,16,72]{0,3,1,2:T(8,128)(2,1)} %copy.10), calls=%async_computation | async-start | bytes 9437184 | tf_op jit(solution)/shard_map/all_to_all | solution.py:25
  88.6 0.0 copy-done.2
  88.7 0.1 mul.76
  88.8 143.3 %all-to-all-done = bf16[128,16,16,72]{0,3,1,2:T(8,128)(2,1)} async-done(((bf16[128,16,16,72]{0,3,1,2:T(8,128)(2,1)}), bf16[128,16,16,72]{0,3,1,2:T(8,128)(2,1)}, u32[]{:S(2)}, u32[]{:S(2)}) %all-to-all-start) | async-done | bytes 4718624 | tf_op jit(solution)/shard_map/all_to_all | solution.py:25
  232.1 7.6 %copy.11 = bf16[16,128,16,1,72]{1,0,4,2,3:T(8,128)(2,1)} copy(bf16[16,128,16,1,72]{1,4,2,0,3:T(8,128)(2,1)} %bitcast.2) | data formatting | bytes 9437184 | tf_op jit(solution)/shard_map/all_to_all | solution.py:25
  239.7 110.0 %all-gather.3.cloned.1.call-done = bf16[2048,2304]{1,0:T(8,128)(2,1)} async-done(((bf16[128,2304]{1,0:T(8,128)(2,1)}), bf16[2048,2304]{1,0:T(8,128)(2,1)}) %all-gather.3.cloned.1.call-update) | async-done | bytes 9437200 | tf_op jit(solution)/shard_map/all_gather | solution.py:29
  349.7 17.3 %multiply_reduce_fusion = (f32[2304]{0:T(1024)S(1)}, f32[1152]{0:T(1024)S(1)}, f32[1152,2304]{1,0:T(8,128)}) fusion(bf16[2048,2304]{1,0:T(8,128)(2,1)} %all-gather.3.cloned.1.call-done, bf16[144,8,16,128]{3,2,1,0:T(8,128)(2,1)} %bitcast.19), kind=kOutput, calls=%fused_computation.3 | convolution fusion | flops 10882249728 | bytes 24786432 | tf_op jit(solution)/shard_map/dot_general | solution.py:27
  367.0 39.1 %psum.21 = f32[1152]{0:T(1024)S(1)} all-reduce(f32[1152]{0:T(1024)S(1)} %get-tuple-element.4), channel_id=1, replica_groups=mesh['dp'=16,'mp'=16] {'mp'}, use_global_device_ids=true, to_apply=%region_1.0 | all-reduce | flops 1152 | bytes 9216 | tf_op jit(solution)/shard_map/psum | solution.py:36
  406.1 0.6 fusion.9
  406.7 0.7 reshape.27
  407.4 64.3 %all-reduce = (f32[]{:T(128)}, f32[2304]{0:T(1024)S(1)}) all-reduce(f32[]{:T(128)} %get-tuple-element.7, f32[2304]{0:T(1024)S(1)} %get-tuple-element.3), channel_id=1, replica_groups=mesh['dp'=16,'mp'=16] {'dp'}, use_global_device_ids=true, to_apply=%region_5.0 | all-reduce | flops 2305 | bytes 18440 | tf_op jit(solution)/shard_map/psum | solution.py:40
  471.7 0.0 copy-done.1
  471.7 0.0 copy-start
  472.4 7.9 %multiply_convert_fusion = bf16[1152,2304]{1,0:T(8,128)(2,1)} fusion(f32[1152,2304]{1,0:T(8,128)} %get-tuple-element.9, f32[]{:T(128)S(6)} %div.36, f32[2304]{0:T(1024)S(1)} %multiply_add_fusion, f32[1152]{0:T(1024)S(1)} %get-tuple-element.8), kind=kLoop, calls=%fused_computation.2 | loop fusion | flops 10616832 | bytes 15939076 | tf_op jit(solution)/shard_map/convert_element_type | solution.py:41
  480.2 0.0 copy-done
  (3 shorter events, 0.0 us)
Async XLA Ops:
  7.2 68.4 %all-gather.5.cloned.1.call-start = ((), (), s32[]{:S(2)}) async-start(), calls=%async_computation.2 | async-start | bytes 5013504 | tf_op jit(solution)/shard_map/all_gather | solution.py:23
  9.1 340.6 %all-gather.3.cloned.1.call-start = ((), (), s32[]{:S(2)}) async-start(), calls=%async_computation.1 | async-start | bytes 10027008 | tf_op jit(solution)/shard_map/all_gather | solution.py:29
  81.3 7.3 %copy-start.2 = (f32[16,72]{1,0:T(8,128)S(1)}, f32[16,72]{1,0:T(8,128)}, u32[]{:S(2)}) copy-start(f32[16,72]{1,0:T(8,128)} %param.6) | copy-start | bytes 13828
  81.3 150.8 %all-to-all-start = ((bf16[128,16,16,72]{0,3,1,2:T(8,128)(2,1)}), bf16[128,16,16,72]{0,3,1,2:T(8,128)(2,1)}, u32[]{:S(2)}, u32[]{:S(2)}) async-start(bf16[128,16,16,72]{0,3,1,2:T(8,128)(2,1)} %copy.10), calls=%async_computation | async-start | bytes 9437184 | tf_op jit(solution)/shard_map/all_to_all | solution.py:25
  349.7 122.0 %copy-start.1 = (f32[2304]{0:T(1024)S(1)}, f32[2304]{0:T(1024)}, u32[]{:S(2)}) copy-start(f32[2304]{0:T(1024)} %param.7) | copy-start | bytes 27652
  471.7 8.5 %copy-start = (f32[2304]{0:T(1024)}, f32[2304]{0:T(1024)S(1)}, u32[]{:S(2)}) copy-start(f32[2304]{0:T(1024)S(1)} %multiply_add_fusion) | copy-start | bytes 27652
Sparse Core Ops, SparseCore 0:
  11.3 64.2 all-gather.4
  77.4 272.3 all-gather.2
where the time goes:
time: 488 us; the launch traced here: 487 us
  waiting for transfers between devices  318 us (65%)
  blocking collectives  103 us (21%)
  matrix products  17.3 us (4%)
  local copies, waits for them, and re-layouts  16 us (3%)
  between operations  14.7 us (3%)
  other arithmetic  10.8 us (2%)
  starting transfers between devices  7.4 us (2%)
    all_to_all x1, waiting for transfers between devices, body(): lax.all_to_all(split_out, 'dp', split_axis=2, concat_axis=0, tiled=True)  143 us
    all_gather x1, waiting for transfers between devices, body(): lax.all_gather(hidden, 'dp', axis=0, tiled=True)  110 us
    psum x1, blocking collectives, body(): scale = lax.psum(jnp.sum(row_new), 'dp') / D  64.3 us
    all_gather x1, waiting for transfers between devices, body(): full_out = lax.all_gather(grad_out, 'mp', axis=1, tiled=True)  64.1 us
    psum x1, blocking collectives, body(): row_sum = lax.psum(jnp.sum(squares, axis=1), 'mp')  39.1 us
    dot_general x1, matrix products, body(): lax.dot_general(own_cols, lax.all_gather(hidden, 'dp', axis=0, tiled=True...  17.3 us
  transfers between devices with their start and end apart: 3, of which 3 were waited for; matrix products, arithmetic and copies ran while one was open for 3% of the time, Pallas kernels for 0%

commit v1 on v0

v1 whole, which is shorter than its diff:
```python
import jax
import jax.numpy as jnp
from jax import lax
from jax.sharding import Mesh, PartitionSpec as P

D = 18432

decay = 1.0 - 2.0 ** (-0.8)
tiny = 1e-30

DP = ("z", "yl")
DPR = ("yl", "z")
MP = ("x", "yh", "core")


def ring(n, s):
    return [(i, (i + s) % n) for i in range(n)]


def gather_mp(q):
    x = lax.axis_index("x")
    yh = lax.axis_index("yh")
    core = lax.axis_index("core")
    n = q.shape[0]
    other = lax.ppermute(q, "yh", ring(2, 1))
    pair = jnp.concatenate([q, other], 0)
    fwd = lax.ppermute(pair, "x", ring(4, 1))
    bwd = lax.ppermute(pair, "x", ring(4, -1))
    far_a = lax.ppermute(fwd[:n], "x", ring(4, 1))
    far_b = lax.ppermute(bwd[n:], "x", ring(4, -1))
    rel = jnp.stack([pair, fwd, jnp.concatenate([far_a, far_b], 0), bwd], 0)
    rel = rel.reshape((4, 2) + q.shape)
    theirs = lax.ppermute(rel, "core", ring(2, 1))
    both = jnp.stack([rel, theirs], 2)
    out = jnp.zeros((4, 2, 2) + q.shape, q.dtype)
    for rx in range(4):
        for ry in range(2):
            for rc in range(2):
                out = lax.dynamic_update_slice(
                    out,
                    both[rx, ry, rc][None, None, None],
                    ((x + 4 - rx) % 4, (yh + ry) % 2, (core + rc) % 2, 0, 0, 0),
                )
    return out.reshape((16,) + q.shape)


def spread_sum(v, axes, n):
    got = lax.all_to_all(jnp.broadcast_to(v[None], (n,) + v.shape), axes, 0, 0, tiled=True)
    return jnp.sum(got, axis=0)


def body(pre_act, grad_out, row_state, col_state):
    tok_rows, hid_cols = pre_act.shape
    all_tokens = tok_rows * 16
    all_hidden = hid_cols * 16
    width = row_state.shape[1]
    own = 16 * width
    hidden = jax.nn.gelu(pre_act.astype(jnp.float32)).astype(jnp.bfloat16)
    parts = 2
    pw = hid_cols // parts
    hid = [
        lax.all_gather(hidden[:, i * pw : (i + 1) * pw], DPR, axis=0, tiled=True)
        for i in range(parts)
    ]
    go = grad_out.T.reshape(8, 2, width, tok_rows).transpose(1, 0, 2, 3)
    go = go.reshape(16, width, tok_rows)
    q = lax.all_to_all(go, DPR, 0, 0, tiled=True)
    allq = gather_mp(q)
    lhs = allq.transpose(0, 2, 1, 3).reshape(own, all_tokens)
    grads = []
    rows = 0.0
    cols = []
    for h in hid:
        g = lax.dot_general(
            lhs, h, (((1,), (0,)), ((), ())), preferred_element_type=jnp.float32
        ) / all_tokens
        s = g * g
        rows = rows + jnp.sum(s, axis=1)
        cols.append(jnp.sum(s, axis=0))
        grads.append(g)
    row_sum = spread_sum(rows.reshape(16, width), MP, 16)
    row_new = decay * row_state + (1.0 - decay) * (row_sum / all_hidden + tiny)
    vec = jnp.concatenate(cols + [jnp.full((256,), jnp.sum(row_new), jnp.float32)])
    got = spread_sum(vec.reshape(20, 128), DP, 16).reshape(-1)
    col_new = decay * col_state + (1.0 - decay) * (got[:hid_cols] / D + tiny)
    scale = got[hid_cols] / D
    ups = []
    for i, g in enumerate(grads):
        c = col_new[i * pw : (i + 1) * pw]
        ups.append(
            (g * lax.rsqrt(row_new.reshape(own)[:, None] * c[None, :] / scale)).astype(
                jnp.bfloat16
            )
        )
    update = jnp.concatenate(ups, 1)
    return update.reshape(16, width, hid_cols), row_new, col_new


def solution(mesh):
    fine = Mesh(mesh.devices.reshape(8, 2, 4, 2, 2), ("z", "yl", "x", "yh", "core"))
    return jax.shard_map(
        body,
        mesh=fine,
        in_specs=(P(DP, MP), P(DP, MP), P(None, DP), P(MP)),
        out_specs=(P(None, DP, MP), P(None, DP), P(MP)),
        check_vma=False,
    )
```

time: 488 us -> 238 us (0.49)
  waiting for transfers between devices: 318 us -> 105 us
  blocking collectives: 103 us -> 35.5 us
  local copies, waits for them, and re-layouts: 16 us -> 30 us
  matrix products: 17.3 us -> 25.7 us
  starting transfers between devices: 7.4 us -> 13.5 us
    all_to_all x1, waiting for transfers between devices: 143 us -> 11.5 us  [spread_sum(): lax.all_to_all(jnp.broadcast_to(v[None], (n,) + v.shape), axes, 0, 0, til...]
    all_gather x2, waiting for transfers between devices: 174 us -> 42.5 us  [body(): lax.all_gather(hidden[:, i * pw:(i + 1) * pw], DPR, axis=0, tiled=True)]
    psum x2 -> x0, blocking collectives: 103 us -> none  [the longest x1 64.3 us: body(): scale = lax.psum(jnp.sum(row_new), 'dp') / D]
    ppermute x0 -> x6, waiting for transfers between devices: none -> 50.9 us  [the longest x1 35.6 us: gather_mp(): other = lax.ppermute(q, 'yh', ring(2, 1))]
    all_to_all x0 -> x2, blocking collectives: none -> 35.5 us  [the longest x1 20.7 us: body(): q = lax.all_to_all(go, DPR, 0, 0, tiled=True)]
    dynamic_update_slice x0 -> x16, local copies, waits for them, and re-layouts: none -> 12.1 us  [gather_mp(): lax.dynamic_update_slice(out, both[rx, ry, rc][None, None, None], ((x + 4...]
    ppermute x0 -> x6, starting transfers between devices: none -> 9.85 us  [the longest x1 2.9 us: gather_mp(): other = lax.ppermute(q, 'yh', ring(2, 1))]
    concatenate x0 -> x3, local copies, waits for them, and re-layouts: none -> 8.63 us  [the longest x1 8.54 us: body(): update = jnp.concatenate(ups, 1)]
  transfers between devices with their start and end apart: 3 -> 9, of which waited for: 3 -> 7; matrix products, arithmetic and copies ran while one was open for 3% -> 14% of each run, Pallas kernels for 0% -> 0%
where the time goes in v1:
time: 238 us; the launch traced here: 236 us
  waiting for transfers between devices  105 us (44%)
  blocking collectives  35.5 us (15%)
  local copies, waits for them, and re-layouts  30 us (13%)
  matrix products  25.7 us (11%)
  between operations  14.9 us (6%)
  starting transfers between devices  13.5 us (6%)
  other arithmetic  11.6 us (5%)
    all_gather x2, waiting for transfers between devices, body(): lax.all_gather(hidden[:, i * pw:(i + 1) * pw], DPR, axis=0, tiled=True)  42.5 us
    ppermute x1, waiting for transfers between devices, gather_mp(): other = lax.ppermute(q, 'yh', ring(2, 1))  35.6 us
    dot_general x2, matrix products, body(): lax.dot_general(lhs, h, (((1,), (0,)), ((), ())), preferred_element_type=...  25.7 us
    all_to_all x1, blocking collectives, body(): q = lax.all_to_all(go, DPR, 0, 0, tiled=True)  20.7 us
    all_to_all x1, blocking collectives, spread_sum(): lax.all_to_all(jnp.broadcast_to(v[None], (n,) + v.shape), axes, 0, 0, til...  14.8 us
    dynamic_update_slice x16, local copies, waits for them, and re-layouts, gather_mp(): lax.dynamic_update_slice(out, both[rx, ry, rc][None, None, None], ((x + 4...  12.1 us
    all_to_all x1, waiting for transfers between devices, spread_sum(): lax.all_to_all(jnp.broadcast_to(v[None], (n,) + v.shape), axes, 0, 0, til...  11.5 us
    ppermute x1, waiting for transfers between devices, gather_mp(): fwd = lax.ppermute(pair, 'x', ring(4, 1))  9.99 us
  transfers between devices with their start and end apart: 9, of which 7 were waited for; matrix products, arithmetic and copies ran while one was open for 14% of the time, Pallas kernels for 0%

profile of v1, /device:TPU:0, one launch (start us, length us, event | category | flops | bytes accessed | tf_op | source)
XLA Modules:
  0.0 236.1 jit_solution(5013837065171571522)
XLA Ops:
  7.2 1.5 fusion.9
  8.7 0.9 fusion.16
  9.6 1.2 copy.46
  10.8 20.7 %all_to_all.15 = bf16[16,72,128]{2,1,0:T(8,128)(2,1)S(1)} all-to-all(bf16[16,72,128]{2,1,0:T(8,128)(2,1)S(1)} %bitcast.49), channel_id=1, replica_groups=mesh['z'=8,'yl'=2,'x'=4,'yh'=2,'core'=2] {'yl','z'}, dimensions={0} | all-to-all | bytes 589824 | tf_op jit(solution)/shard_map/all_to_all | solution.py:67
  31.6 2.9 %collective-permute-start = (bf16[16,72,128]{2,1,0:T(8,128)(2,1)S(1)}, bf16[16,72,128]{2,1,0:T(8,128)(2,1)S(1)}, u32[]{:S(2)}, u32[]{:S(2)}) collective-permute-start(bf16[16,72,128]{2,1,0:T(8,128)(2,1)S(1)} %all_to_all.15), channel_id=1, source_target_pairs={{0,2},{2,0},{1,3},{3,1},{4,6},{6,4},{5,7},{7,5},{8,10},{10,8},{9,1... | collective-permute-start | bytes 884744 | tf_op jit(solution)/shard_map/ppermute | solution.py:25
  34.5 35.6 %collective-permute-done = bf16[16,72,128]{2,1,0:T(8,128)(2,1)S(1)} collective-permute-done((bf16[16,72,128]{2,1,0:T(8,128)(2,1)S(1)}, bf16[16,72,128]{2,1,0:T(8,128)(2,1)S(1)}, u32[]{:S(2)}, u32[]{:S(2)}) %collective-permute-start) | collective-permute-done | bytes 294944 | tf_op jit(solution)/shard_map/ppermute | solution.py:25
  70.2 1.2 collective-permute-start.1
  71.4 2.2 collective-permute-start.3
  73.6 10.0 %collective-permute-done.1 = bf16[32,72,128]{2,1,0:T(8,128)(2,1)S(1)} collective-permute-done((bf16[32,72,128]{2,1,0:T(8,128)(2,1)S(1)}, bf16[32,72,128]{2,1,0:T(8,128)(2,1)S(1)}, u32[]{:S(2)}, u32[]{:S(2)}) %collective-permute-start.1) | collective-permute-done | bytes 589856 | tf_op jit(solution)/shard_map/ppermute | solution.py:27
  84.5 2.8 %collective-permute-start.4 = (bf16[16,72,128]{2,1,0:T(8,128)(2,1)S(1)}, bf16[16,72,128]{2,1,0:T(8,128)(2,1)S(1)}, u32[]{:S(2)}, u32[]{:S(2)}) collective-permute-start(bf16[16,72,128]{2,1,0:T(8,128)(2,1)S(1)} %slice.107), channel_id=1, source_target_pairs={{0,12},{4,0},{8,4},{12,8},{1,13},{5,1},{9,5},{13,9},{2,14},{6,2},{... | collective-permute-start | bytes 884744 | tf_op jit(solution)/shard_map/ppermute | solution.py:30
  87.3 4.3 %collective-permute-done.2 = bf16[16,72,128]{2,1,0:T(8,128)(2,1)S(1)} collective-permute-done((bf16[16,72,128]{2,1,0:T(8,128)(2,1)S(1)}, bf16[16,72,128]{2,1,0:T(8,128)(2,1)S(1)}, u32[]{:S(2)}, u32[]{:S(2)}) %collective-permute-start.2) | collective-permute-done | bytes 294944 | tf_op jit(solution)/shard_map/ppermute | solution.py:29
  91.7 1.7 pad_maximum_fusion.1
  93.4 3.0 %broadcast_in_dim.20 = bf16[4,2,2,16,72,128]{5,3,4,2,1,0:T(8,128)(2,1)} broadcast(bf16[]{:T(256)} %constant.161.clone.1), dimensions={} | broadcast | bytes 4718594 | tf_op jit(solution)/shard_map/broadcast_in_dim | solution.py:35
  97.4 0.8 collective-permute-done.5
  98.3 1.8 fusion.15
  111.4 12.7 %multiply_reduce_fusion = (f32[1152]{0:T(1024)S(1)}, f32[1152]{0:T(1024)S(1)}, f32[1152,1152]{0,1:T(8,128)}) fusion(bf16[2048,1152]{1,0:T(8,128)(2,1)} %all-gather.5.cloned.1.call-done, bf16[144,8,16,128]{3,2,1,0:T(8,128)(2,1)} %bitcast.24), kind=kOutput, calls=%fused_computation.5 | convolution fusion | flops 5441124352 | bytes 14754816 | tf_op jit(solution)/shard_map/dot_general | solution.py:74
  124.1 42.5 %all-gather.3.cloned.1.call-done = bf16[2048,1152]{1,0:T(8,128)(2,1)} async-done(((bf16[128,1152]{1,0:T(8,128)(2,1)}), bf16[2048,1152]{1,0:T(8,128)(2,1)}) %all-gather.3.cloned.1.call-update) | async-done | bytes 4718608 | tf_op jit(solution)/shard_map/all_gather | solution.py:62
  166.7 13.0 %multiply_reduce_fusion.2 = (f32[1152]{0:T(1024)S(1)}, f32[1152]{0:T(1024)S(1)}, f32[1152,1152]{0,1:T(8,128)}) fusion(bf16[2048,1152]{1,0:T(8,128)(2,1)} %all-gather.3.cloned.1.call-done, bf16[144,8,16,128]{3,2,1,0:T(8,128)(2,1)} %bitcast.24), kind=kOutput, calls=%fused_computation.7 | convolution fusion | flops 5441124352 | bytes 14754816 | tf_op jit(solution)/shard_map/dot_general | solution.py:74
  179.7 14.8 %all_to_all.16 = f32[16,16,72]{2,1,0:T(8,128)S(1)} all-to-all(f32[16,16,72]{2,1,0:T(8,128)S(1)} %broadcast_in_dim.21), channel_id=1, replica_groups=mesh['z'=8,'yl'=2,'x'=4,'yh'=2,'core'=2] {'x','yh','core'}, dimensions={0} | all-to-all | bytes 147456 | tf_op jit(solution)/shard_map/all_to_all | solution.py:48
  196.6 3.6 %all-to-all-start.2 = ((f32[16,20,128]{2,1,0:T(8,128)}), f32[16,20,128]{2,1,0:T(8,128)S(1)}, u32[]{:S(2)}, u32[]{:S(2)}) async-start(f32[16,20,128]{2,1,0:T(8,128)} %broadcast_in_dim.24), calls=%async_computation.2 | async-start | bytes 393216 | tf_op jit(solution)/shard_map/all_to_all | solution.py:48
  200.3 11.5 %all-to-all-done.2 = f32[16,20,128]{2,1,0:T(8,128)S(1)} async-done(((f32[16,20,128]{2,1,0:T(8,128)}), f32[16,20,128]{2,1,0:T(8,128)S(1)}, u32[]{:S(2)}, u32[]{:S(2)}) %all-to-all-start.2) | async-done | bytes 163872 | tf_op jit(solution)/shard_map/all_to_all | solution.py:48
  213.0 5.0 %multiply_convert_fusion.1 = (bf16[1152,1152]{0,1:T(8,128)(2,1)S(1)}, bf16[1152,1152]{0,1:T(8,128)(2,1)S(1)}) fusion(f32[1152,1152]{0,1:T(8,128)} %get-tuple-element.34, f32[]{:T(128)} %bitcast.18, f32[1152]{0:T(1024)S(1)} %get-tuple-element.30, f32[1152]{0:T(1024)S(1)} %mul.99, f32[1152,1152]{0,1:T(8,128)} %get-tuple-element.35, f32[1152]{0:T(1024)S(1)} %get-tuple-element.31), kind=kLoop, calls=%fused_computation.4 | loop fusion | flops 10616832 | bytes 15939076 | tf_op jit(solution)/shard_map/convert_element_type | solution.py:91
  218.0 2.7 %pad_maximum_fusion = bf16[1152,2304]{0,1:T(8,128)(2,1)} fusion(bf16[1152,1152]{0,1:T(8,128)(2,1)S(1)} %get-tuple-element.33, bf16[1152,1152]{0,1:T(8,128)(2,1)S(1)} %get-tuple-element.32), kind=kLoop, calls=%fused_computation.2 | loop fusion | flops 10616832 | bytes 10616832 | tf_op jit(solution)/shard_map/concatenate | solution.py:95
  220.8 8.5 %copy.65 = bf16[1152,2304]{1,0:T(8,128)(2,1)} copy(bf16[1152,2304]{0,1:T(8,128)(2,1)} %pad_maximum_fusion) | data formatting | bytes 10616832 | tf_op jit(solution)/shard_map/concatenate | solution.py:95
  (57 shorter events, 16.3 us)
Async XLA Ops:
  7.2 104.2 %all-gather.5.cloned.1.call-start = ((), (), s32[]{:S(2)}) async-start(), calls=%async_computation.4 | async-start | bytes 5013504 | tf_op jit(solution)/shard_map/all_gather | solution.py:62
  9.6 157.1 %all-gather.3.cloned.1.call-start = ((), (), s32[]{:S(2)}) async-start(), calls=%async_computation.3 | async-start | bytes 5013504 | tf_op jit(solution)/shard_map/all_gather | solution.py:62
  31.6 38.5 %collective-permute-start = (bf16[16,72,128]{2,1,0:T(8,128)(2,1)S(1)}, bf16[16,72,128]{2,1,0:T(8,128)(2,1)S(1)}, u32[]{:S(2)}, u32[]{:S(2)}) collective-permute-start(bf16[16,72,128]{2,1,0:T(8,128)(2,1)S(1)} %all_to_all.15), channel_id=1, source_target_pairs={{0,2},{2,0},{1,3},{3,1},{4,6},{6,4},{5,7},{7,5},{8,10},{10,8},{9,1... | collective-permute-start | bytes 884744 | tf_op jit(solution)/shard_map/ppermute | solution.py:25
  70.2 13.4 %collective-permute-start.1 = (bf16[32,72,128]{2,1,0:T(8,128)(2,1)S(1)}, bf16[32,72,128]{2,1,0:T(8,128)(2,1)S(1)}, u32[]{:S(2)}, u32[]{:S(2)}) collective-permute-start(bf16[32,72,128]{2,1,0:T(8,128)(2,1)S(1)} %constant_dynamic-update-slice_fusion), channel_id=1, source_target_pairs={{0,4},{4,8},{8,12},{12,0},{1,5},{5,9},{9,13},{13,1},{2,6},{6,10},{... | collective-permute-start | bytes 1769480 | tf_op jit(solution)/shard_map/ppermute | solution.py:27
  71.4 13.1 %collective-permute-start.3 = (bf16[32,72,128]{2,1,0:T(8,128)(2,1)S(1)}, bf16[32,72,128]{2,1,0:T(8,128)(2,1)S(1)}, u32[]{:S(2)}, u32[]{:S(2)}) collective-permute-start(bf16[32,72,128]{2,1,0:T(8,128)(2,1)S(1)} %constant_dynamic-update-slice_fusion), channel_id=1, source_target_pairs={{0,12},{4,0},{8,4},{12,8},{1,13},{5,1},{9,5},{13,9},{2,14},{6,2},{... | collective-permute-start | bytes 1769480 | tf_op jit(solution)/shard_map/ppermute | solution.py:28
  83.6 8.0 %collective-permute-start.2 = (bf16[16,72,128]{2,1,0:T(8,128)(2,1)S(1)}, bf16[16,72,128]{2,1,0:T(8,128)(2,1)S(1)}, u32[]{:S(2)}, u32[]{:S(2)}) collective-permute-start(bf16[16,72,128]{2,1,0:T(8,128)(2,1)S(1)} %slice.106), channel_id=1, source_target_pairs={{0,4},{4,8},{8,12},{12,0},{1,5},{5,9},{9,13},{13,1},{2,6},{6,10},{... | collective-permute-start | bytes 884744 | tf_op jit(solution)/shard_map/ppermute | solution.py:29
  84.5 7.1 %collective-permute-start.4 = (bf16[16,72,128]{2,1,0:T(8,128)(2,1)S(1)}, bf16[16,72,128]{2,1,0:T(8,128)(2,1)S(1)}, u32[]{:S(2)}, u32[]{:S(2)}) collective-permute-start(bf16[16,72,128]{2,1,0:T(8,128)(2,1)S(1)} %slice.107), channel_id=1, source_target_pairs={{0,12},{4,0},{8,4},{12,8},{1,13},{5,1},{9,5},{13,9},{2,14},{6,2},{... | collective-permute-start | bytes 884744 | tf_op jit(solution)/shard_map/ppermute | solution.py:30
  93.4 4.9 %collective-permute-start.5 = (bf16[4,2,16,72,128]{4,3,2,1,0:T(8,128)(2,1)}, bf16[4,2,16,72,128]{4,3,2,1,0:T(8,128)(2,1)}, u32[]{:S(2)}, u32[]{:S(2)}) collective-permute-start(bf16[4,2,16,72,128]{4,3,2,1,0:T(8,128)(2,1)} %pad_maximum_fusion.1), channel_id=1, source_target_pairs={{0,1},{1,0},{2,3},{3,2},{4,5},{5,4},{6,7},{7,6},{8,9},{9,8},{10,11... | collective-permute-start | bytes 7077896 | tf_op jit(solution)/shard_map/ppermute | solution.py:33
  124.1 70.4 %copy-start.3 = (f32[16,72]{1,0:T(8,128)S(1)}, f32[16,72]{1,0:T(8,128)}, u32[]{:S(2)}) copy-start(f32[16,72]{1,0:T(8,128)} %param.6) | copy-start | bytes 13828
  124.1 87.6 %copy-start.2 = (f32[2304]{0:T(1024)S(1)}, f32[2304]{0:T(1024)}, u32[]{:S(2)}) copy-start(f32[2304]{0:T(1024)} %param.7) | copy-start | bytes 27652
  195.2 22.8 %copy-start.1 = (f32[16,72]{1,0:T(8,128)}, f32[16,72]{1,0:T(8,128)S(1)}, u32[]{:S(2)}) copy-start(f32[16,72]{1,0:T(8,128)S(1)} %get-tuple-element.11) | copy-start | bytes 13828
  196.6 15.2 %all-to-all-start.2 = ((f32[16,20,128]{2,1,0:T(8,128)}), f32[16,20,128]{2,1,0:T(8,128)S(1)}, u32[]{:S(2)}, u32[]{:S(2)}) async-start(f32[16,20,128]{2,1,0:T(8,128)} %broadcast_in_dim.24), calls=%async_computation.2 | async-start | bytes 393216 | tf_op jit(solution)/shard_map/all_to_all | solution.py:48
  211.8 6.2 %copy-start = (f32[2304]{0:T(1024)}, f32[2304]{0:T(1024)S(1)}, u32[]{:S(2)}) copy-start(f32[2304]{0:T(1024)S(1)} %fusion.13) | copy-start | bytes 27652
Sparse Core Ops, SparseCore 0:
  9.8 81.0 all-gather.4
  92.7 73.9 all-gather.2

commit v2 on v0

v2 whole, which is shorter than its diff:
```python
import functools

import jax
import jax.numpy as jnp
from jax import lax
from jax.experimental import pallas as pl
from jax.experimental.pallas import tpu as pltpu
from jax.sharding import Mesh, PartitionSpec as P

D = 18432

decay = 1.0 - 2.0 ** (-0.8)
tiny = 1e-30

DP = ("z", "yl")
MP = ("x", "yh", "core")

TOK = 128
HID = 2304
WID = 72
OWN = 1152
ALL_TOK = 2048
FFW = 36864
CB = 256
A_COLS = 1536
A_BLOCKS = A_COLS // CB
BLOCKS = HID // CB
A_HALF = A_COLS // 2
SPLIT = 1024
MIB = 1024 * 1024

ANY = pl.BlockSpec(memory_space=pl.ANY)
VMEM = pl.BlockSpec(memory_space=pltpu.VMEM)
SMEM = pl.BlockSpec(memory_space=pltpu.SMEM)


def ring(n, s):
    return [(i, (i + s) % n) for i in range(n)]


def send(v, axis, n, s):
    return lax.ppermute(v, axis, ring(n, s))


def lhs_kernel(pos, xp, f, b, fa, fb, cxp, cf, cb, cfa, cfb, out):
    x, yh, core = pos[2], pos[3], pos[4]
    for half, group in ((core, (xp, f, b, fa, fb)), (1 - core, (cxp, cf, cb, cfa, cfb))):
        gxp, gf, gb, gfa, gfb = group
        for ref, lead, dx, dy in (
            (gxp, 0, 0, 0),
            (gxp, 1, 0, 1),
            (gf, 0, 3, 0),
            (gf, 1, 3, 1),
            (gb, 0, 1, 0),
            (gb, 1, 1, 1),
            (gfa, None, 2, 0),
            (gfb, None, 2, 1),
        ):
            row = (lax.rem(x + dx, 4) * 2 + lax.rem(yh + dy, 2)) * (2 * WID)
            row = pl.multiple_of(row, 16)
            for i in range(8):
                block = ref[i] if lead is None else ref[lead, i]
                col = pl.multiple_of((half * 8 + i) * TOK, TOK)
                out[pl.ds(row, 2 * WID), pl.ds(col, TOK)] = block


def place_features(pos, mine, theirs):
    return pl.pallas_call(
        lhs_kernel,
        out_shape=jax.ShapeDtypeStruct((OWN, ALL_TOK), jnp.bfloat16),
        in_specs=[SMEM] + [VMEM] * 10,
        out_specs=VMEM,
        compiler_params=pltpu.CompilerParams(vmem_limit_bytes=50 * MIB),
        cost_estimate=pl.CostEstimate(
            flops=0, bytes_accessed=2 * OWN * ALL_TOK * 2, transcendentals=0
        ),
        name="features",
    )(pos, *mine, *theirs)


def tie(*v):
    return lax.optimization_barrier(v)


def up_z(v):
    return send(v, "z", 8, 1)


def down_z(v):
    return send(v, "z", 8, -1)


def other(v, axis):
    return send(v, axis, 2, 1)


def exchange(hidden, grad_out, pos):
    core = pos[4]

    def cross(*parts):
        return other(jnp.concatenate(parts, 0), "yl")

    def cut(v, first, last):
        return lax.slice_in_dim(v, first, last, axis=1)

    hidden, grad_out = tie(hidden, grad_out)
    u1, d1, near = up_z(hidden), down_z(hidden), other(hidden, "yl")
    turned = grad_out.T.reshape(16, WID, TOK)
    q = lax.all_to_all(turned, DP, 0, 0, tiled=True)
    u1, d1, near = tie(u1, d1, near)
    side = cut(near, 0, A_COLS)
    u2 = up_z(jnp.concatenate([u1, side], 1))
    d2 = down_z(jnp.concatenate([d1, side], 1))
    y1 = cross(cut(u1, A_COLS, HID), cut(d1, A_COLS, HID))
    keep = lax.dynamic_slice_in_dim(q, 8 * core, 8, 0)
    give = lax.dynamic_slice_in_dim(q, 8 - 8 * core, 8, 0)
    got = other(give, "core")
    first = jnp.where(core == 0, keep, got)
    second = jnp.where(core == 0, got, keep)
    half = jnp.concatenate([first, second], 1)
    far = other(half, "yh")
    u2, d2, y1, far = tie(u2, d2, y1, far)
    u3, d3 = up_z(u2), down_z(d2)
    xp = jnp.stack([half, far], 0)
    f, b = send(xp, "x", 4, 1), send(xp, "x", 4, -1)
    y2 = cross(cut(u2, A_COLS, HID), cut(d2, A_COLS, HID))
    cxp = other(xp, "core")
    u3, d3, y2, f, b, cxp = tie(u3, d3, y2, f, b, cxp)
    u4 = up_z(jnp.concatenate([cut(u3, 0, SPLIT), cut(u3, HID, HID + A_COLS)], 1))
    d4 = down_z(cut(d3, SPLIT, HID + A_COLS))
    fa, fb = send(f[0], "x", 4, 1), send(b[1], "x", 4, -1)
    cf, cb = other(f, "core"), other(b, "core")
    y3 = cross(cut(u3, A_COLS, HID), cut(d3, A_COLS, HID))
    u4, d4, y3, fa, fb, cf, cb = tie(u4, d4, y3, fa, fb, cf, cb)
    u5 = up_z(cut(u4, SPLIT, SPLIT + A_HALF))
    d5 = down_z(cut(d4, HID - SPLIT + A_HALF, HID - SPLIT + A_COLS))
    y4 = cross(cut(d4, A_COLS - SPLIT, HID - SPLIT))
    lhs = place_features(
        pos, (xp, f, b, fa, fb), (cxp, cf, cb, other(fa, "core"), other(fb, "core"))
    )
    n, m, h, k = BLOCKS, A_BLOCKS, SPLIT // CB, A_HALF // CB
    pieces = [
        (hidden, 0, 0, 0, 0, 0, n),
        (near, 0, 0, 0, 1, 0, n),
        (u1, 0, 0, 7, 0, 0, n),
        (d1, 0, 0, 1, 0, 0, n),
        (y1, 0, -A_COLS, 7, 1, m, n),
        (y1, TOK, -A_COLS, 1, 1, m, n),
        (u2, 0, 0, 6, 0, 0, n),
        (d2, 0, 0, 2, 0, 0, n),
        (u2, 0, HID, 7, 1, 0, m),
        (d2, 0, HID, 1, 1, 0, m),
        (y2, 0, -A_COLS, 6, 1, m, n),
        (y2, TOK, -A_COLS, 2, 1, m, n),
        (u3, 0, 0, 5, 0, 0, n),
        (d3, 0, 0, 3, 0, 0, n),
        (u3, 0, HID, 6, 1, 0, m),
        (d3, 0, HID, 2, 1, 0, m),
        (y3, 0, -A_COLS, 5, 1, m, n),
        (y3, TOK, -A_COLS, 3, 1, m, n),
        (u4, 0, 0, 4, 0, 0, h),
        (d4, 0, -SPLIT, 4, 0, h, n),
        (u4, 0, SPLIT, 5, 1, 0, m),
        (d4, 0, HID - SPLIT, 3, 1, 0, m),
        (y4, 0, -A_COLS, 4, 1, m, n),
        (u5, 0, 0, 4, 1, 0, k),
        (d5, 0, -A_HALF, 4, 1, k, m),
    ]
    return pieces, lhs


def product_kernel(plan, count, pos, lhs_hbm, *refs):
    arrays = refs[:count]
    grad, rows_out, cols_out = refs[count : count + 3]
    lhs, hid, outbuf, rowacc, lsem, hsem, osem = refs[count + 3 :]
    z, yl = pos[0], pos[1]

    def issue(j, slot):
        edges = sorted({p[5] for p in plan} | {p[6] for p in plan})
        for lo, hi in zip(edges[:-1], edges[1:]):

            @pl.when((j >= lo) & (j < hi))
            def _(lo=lo):
                for index, row, base, dz, dy, first, last in plan:
                    if not first <= lo < last:
                        continue
                    s = lax.rem(z + dz, 8) * 2 + lax.rem(yl + dy, 2)
                    col = pl.multiple_of(j * CB + base, CB)
                    pltpu.make_async_copy(
                        arrays[index].at[pl.ds(row, TOK), pl.ds(col, CB)],
                        hid.at[slot, pl.ds(pl.multiple_of(s * TOK, TOK), TOK), :],
                        hsem.at[slot],
                    ).start()

    pltpu.make_async_copy(lhs_hbm, lhs, lsem).start()
    issue(jnp.int32(0), 0)
    rowacc[...] = jnp.zeros_like(rowacc)
    pltpu.make_async_copy(lhs_hbm, lhs, lsem).wait()

    def out_copy(j, slot):
        return pltpu.make_async_copy(
            outbuf.at[slot],
            grad.at[:, pl.ds(pl.multiple_of(j * CB, CB), CB)],
            osem.at[slot],
        )

    def step(j, carry):
        slot = lax.rem(j, 2)

        @pl.when(j + 1 < BLOCKS)
        def _():
            issue(j + 1, 1 - slot)

        pltpu.make_async_copy(hid.at[slot], hid.at[slot], hsem.at[slot]).wait()

        @pl.when(j >= 2)
        def _():
            out_copy(j - 2, slot).wait()

        col = jnp.zeros((8, CB), jnp.float32)
        for r in range(0, OWN, 384):
            g = jnp.dot(
                lhs[r : r + 384, :], hid[slot], preferred_element_type=jnp.float32
            ) * (1.0 / ALL_TOK)
            outbuf[slot, r : r + 384, :] = g
            sq = g * g
            rowacc[r : r + 384, :] += sq[:, :128] + sq[:, 128:]
            col = col + jnp.sum(sq.reshape(48, 8, CB), axis=0)
        total = jnp.sum(col, axis=0, keepdims=True)
        cols_out[pl.ds(2 * j, 1), :] = total[:, :128]
        cols_out[pl.ds(2 * j + 1, 1), :] = total[:, 128:]
        out_copy(j, slot).start()
        return carry

    lax.fori_loop(0, BLOCKS, step, 0)
    for i in range(9):
        part = rowacc[i * 128 : (i + 1) * 128, :]
        line = jnp.sum(part.T, axis=0, keepdims=True)
        for d in range(16):
            rows_out[d, i : i + 1, :] = line
    out_copy(BLOCKS - 2, (BLOCKS - 2) % 2).wait()
    out_copy(BLOCKS - 1, (BLOCKS - 1) % 2).wait()


def product(lhs, pieces, pos):
    arrays = []
    plan = []
    for piece in pieces:
        index = [i for i, a in enumerate(arrays) if a is piece[0]]
        if not index:
            arrays.append(piece[0])
            index = [len(arrays) - 1]
        plan.append((index[0],) + piece[1:])
    return pl.pallas_call(
        functools.partial(product_kernel, plan, len(arrays)),
        out_shape=(
            jax.ShapeDtypeStruct((OWN, HID), jnp.float32),
            jax.ShapeDtypeStruct((16, 9, 128), jnp.float32),
            jax.ShapeDtypeStruct((18, 128), jnp.float32),
        ),
        in_specs=[SMEM] + [ANY] * (1 + len(arrays)),
        out_specs=(ANY, VMEM, VMEM),
        scratch_shapes=[
            pltpu.VMEM((OWN, ALL_TOK), jnp.bfloat16),
            pltpu.VMEM((2, ALL_TOK, CB), jnp.bfloat16),
            pltpu.VMEM((2, OWN, CB), jnp.float32),
            pltpu.VMEM((OWN, 128), jnp.float32),
            pltpu.SemaphoreType.DMA,
            pltpu.SemaphoreType.DMA((2,)),
            pltpu.SemaphoreType.DMA((2,)),
        ],
        compiler_params=pltpu.CompilerParams(vmem_limit_bytes=50 * MIB),
        cost_estimate=pl.CostEstimate(
            flops=2 * OWN * HID * ALL_TOK,
            bytes_accessed=OWN * HID * 4 + ALL_TOK * HID * 2,
            transcendentals=0,
        ),
        name="product",
    )(pos, lhs, *arrays)


def middle_kernel(got, row_state, cols, row_new, payload):
    row_sum = jnp.sum(got[...], axis=0)
    new = decay * row_state[...] + (1.0 - decay) * (row_sum / FFW + tiny)
    row_new[...] = new
    total = jnp.sum(jnp.sum(new, axis=0, keepdims=True), axis=1, keepdims=True)
    for d in range(16):
        payload[d, :18, :] = cols[...]
        payload[d, 18:, :] = jnp.broadcast_to(total, (6, 128))


STRIPES = 9


def update_kernel(got, row_new, col_state, grad, out, col_new, colf, gbuf, obuf, rsem, wsem):
    def read(i):
        rows = pl.ds(i * 128, 128)
        return pltpu.make_async_copy(grad.at[rows, :], gbuf.at[rows, :], rsem.at[i])

    def write(i):
        rows = pl.ds(i * 128, 128)
        return pltpu.make_async_copy(obuf.at[rows, :], out.at[rows, :], wsem.at[i])

    for i in range(STRIPES):
        read(i).start()
    sums = jnp.sum(got[...], axis=0)
    new = decay * col_state[...] + (1.0 - decay) * (sums[:18, :] / D + tiny)
    col_new[...] = new
    inv = lax.rsqrt(new)
    for k in range(18):
        colf[:, k * 128 : (k + 1) * 128] = jnp.broadcast_to(inv[k : k + 1, :], (8, 128))
    scale = sums[18:19, :] / D
    rowf = lax.rsqrt(row_new[...]) * jnp.sqrt(scale)
    for i in range(STRIPES):
        column = jnp.broadcast_to(rowf[i : i + 1, :], (128, 128)).T
        read(i).wait()
        for k in range(18):
            sl = slice(k * 128, (k + 1) * 128)
            obuf[i * 128 : (i + 1) * 128, sl] = (
                gbuf[i * 128 : (i + 1) * 128, sl] * (column * colf[0:1, sl])
            ).astype(jnp.bfloat16)
        write(i).start()
    for i in range(STRIPES):
        write(i).wait()


def spread(v, axes):
    return lax.all_to_all(v, axes, 0, 0, tiled=True)


def body(pre_act, grad_out, row_state, col_state):
    pos = jnp.stack([lax.axis_index(a) for a in ("z", "yl", "x", "yh", "core")]).astype(
        jnp.int32
    )
    hidden = jax.nn.gelu(pre_act.astype(jnp.float32)).astype(jnp.bfloat16)
    pieces, lhs = exchange(hidden, grad_out, pos)
    grad, rows, cols = product(lhs, pieces, pos)
    row_new, payload = pl.pallas_call(
        middle_kernel,
        out_shape=(
            jax.ShapeDtypeStruct((9, 128), jnp.float32),
            jax.ShapeDtypeStruct((16, 24, 128), jnp.float32),
        ),
        in_specs=[VMEM] * 3,
        out_specs=(VMEM, VMEM),
        compiler_params=pltpu.CompilerParams(vmem_limit_bytes=4 * MIB),
        name="middle",
    )(spread(rows, MP), row_state.reshape(9, 128), cols)
    update, col_new = pl.pallas_call(
        update_kernel,
        out_shape=(
            jax.ShapeDtypeStruct((OWN, HID), jnp.bfloat16),
            jax.ShapeDtypeStruct((18, 128), jnp.float32),
        ),
        in_specs=[VMEM, VMEM, VMEM, ANY],
        out_specs=(ANY, VMEM),
        scratch_shapes=[
            pltpu.VMEM((8, HID), jnp.float32),
            pltpu.VMEM((OWN, HID), jnp.float32),
            pltpu.VMEM((OWN, HID), jnp.bfloat16),
            pltpu.SemaphoreType.DMA((STRIPES,)),
            pltpu.SemaphoreType.DMA((STRIPES,)),
        ],
        compiler_params=pltpu.CompilerParams(vmem_limit_bytes=50 * MIB),
        name="update",
    )(spread(payload, DP), row_new, col_state.reshape(18, 128), grad)
    return (
        update.reshape(16, WID, HID),
        row_new.reshape(16, WID),
        col_new.reshape(HID),
    )


def solution(mesh):
    fine = Mesh(mesh.devices.reshape(8, 2, 4, 2, 2), ("z", "yl", "x", "yh", "core"))
    return jax.shard_map(
        body,
        mesh=fine,
        in_specs=(P(DP, MP), P(DP, MP), P(None, DP), P(MP)),
        out_specs=(P(None, DP, MP), P(None, DP), P(MP)),
        check_vma=False,
    )
```

time: 488 us -> 170 us (0.35)
  waiting for transfers between devices: 318 us -> 76.6 us
  blocking collectives: 103 us -> 0 us
  starting transfers between devices: 7.4 us -> 47.8 us
  Pallas kernels: 0 us -> 31.5 us
  matrix products: 17.3 us -> 0 us
  between operations: 14.7 us -> 1.13 us
  local copies, waits for them, and re-layouts: 16 us -> 8.3 us
  other arithmetic: 10.8 us -> 3.33 us
    all_gather x2 -> x0, waiting for transfers between devices: 174 us -> none  [the longest x1 110 us: body(): lax.all_gather(hidden, 'dp', axis=0, tiled=True)]
    all_to_all x1 -> x3, waiting for transfers between devices: 143 us -> 18.3 us  [the longest x2 18.3 us: spread(): return lax.all_to_all(v, axes, 0, 0, tiled=True)]
    psum x2 -> x0, blocking collectives: 103 us -> none  [the longest x1 64.3 us: body(): scale = lax.psum(jnp.sum(row_new), 'dp') / D]
    ppermute x0 -> x26, waiting for transfers between devices: none -> 58.3 us  [send(): return lax.ppermute(v, axis, ring(n, s))]
    ppermute x0 -> x26, starting transfers between devices: none -> 32.5 us  [send(): return lax.ppermute(v, axis, ring(n, s))]
    pallas_call x0 -> x4, Pallas kernels: none -> 31.5 us  [the longest x1 18.3 us: product(): pl.pallas_call(functools.partial(product_kernel, plan, len(arrays)), out_...]
    dot_general x1 -> x0, matrix products: 17.3 us -> none  [body(): lax.dot_general(own_cols, lax.all_gather(hidden, 'dp', axis=0, tiled=True...]
    all_to_all x1 -> x3, starting transfers between devices: 7.32 us -> 15.3 us  [the longest x2 9.44 us: spread(): return lax.all_to_all(v, axes, 0, 0, tiled=True)]
  transfers between devices with their start and end apart: 3 -> 29, of which waited for: 3 -> 12; matrix products, arithmetic and copies ran while one was open for 3% -> 3% of each run, Pallas kernels for 0% -> 3%
where the time goes in v2:
time: 170 us; the launch traced here: 169 us
  waiting for transfers between devices  76.6 us (45%)
  starting transfers between devices  47.8 us (28%)
  Pallas kernels  31.5 us (19%)
  local copies, waits for them, and re-layouts  8.3 us (5%)
  other arithmetic  3.33 us (2%)
    ppermute x26, waiting for transfers between devices, send(): return lax.ppermute(v, axis, ring(n, s))  58.3 us
    ppermute x26, starting transfers between devices, send(): return lax.ppermute(v, axis, ring(n, s))  32.5 us
    pallas_call x1, Pallas kernels, product(): pl.pallas_call(functools.partial(product_kernel, plan, len(arrays)), out_...  18.3 us
    all_to_all x2, waiting for transfers between devices, spread(): return lax.all_to_all(v, axes, 0, 0, tiled=True)  18.3 us
    all_to_all x2, starting transfers between devices, spread(): return lax.all_to_all(v, axes, 0, 0, tiled=True)  9.44 us
    pallas_call x1, Pallas kernels, body(): pl.pallas_call(update_kernel, out_shape=(jax.ShapeDtypeStruct((OWN, HID),...  7.04 us
    all_to_all x1, starting transfers between devices, exchange(): q = lax.all_to_all(turned, DP, 0, 0, tiled=True)  5.86 us
    pallas_call x1, Pallas kernels, place_features(): pl.pallas_call(lhs_kernel, out_shape=jax.ShapeDtypeStruct((OWN, ALL_TOK),...  5.3 us
  transfers between devices with their start and end apart: 29, of which 12 were waited for; matrix products, arithmetic and copies ran while one was open for 3% of the time, Pallas kernels for 3%

profile of v2, /device:TPU:0, one launch (start us, length us, event | category | flops | bytes accessed | tf_op | source)
XLA Modules:
  0.0 168.6 jit_solution(4577501907581964038)
XLA Ops:
  2.4 4.0 %collective-permute-start.2 = (bf16[128,2304]{1,0:T(8,128)(2,1)S(1)}, bf16[128,2304]{1,0:T(8,128)(2,1)S(1)}, u32[]{:S(2)}, u32[]{:S(2)}) collective-permute-start(bf16[128,2304]{1,0:T(8,128)(2,1)S(1)} %fusion.5.refs_0_), channel_id=1, source_target_pairs={{0,224},{32,0},{64,32},{96,64},{128,96},{160,128},{192,160},{224,1... | collective-permute-start | bytes 1769480 | tf_op jit(solution)/shard_map/ppermute | solution.py:42
  8.9 5.9 %all-to-all-start = ((bf16[16,72,128]{2,1,0:T(8,128)(2,1)}), bf16[16,72,128]{2,1,0:T(8,128)(2,1)S(1)}, u32[]{:S(2)}, u32[]{:S(2)}) async-start(bf16[16,72,128]{2,1,0:T(8,128)(2,1)} %bitcast.6), calls=%async_computation | async-start | bytes 589824 | tf_op jit(solution)/shard_map/all_to_all | solution.py:109
  14.8 6.4 %collective-permute-done.1.refs_2_ = bf16[128,2304]{1,0:T(8,128)(2,1)S(1)} collective-permute-done((bf16[128,2304]{1,0:T(8,128)(2,1)S(1)}, bf16[128,2304]{1,0:T(8,128)(2,1)S(1)}, u32[]{:S(2)}, u32[]{:S(2)}) %collective-permute-start.1) | collective-permute-done | bytes 589856 | tf_op jit(solution)/shard_map/ppermute | solution.py:42
  21.2 2.8 %collective-permute-done.2.refs_3_ = bf16[128,2304]{1,0:T(8,128)(2,1)S(1)} collective-permute-done((bf16[128,2304]{1,0:T(8,128)(2,1)S(1)}, bf16[128,2304]{1,0:T(8,128)(2,1)S(1)}, u32[]{:S(2)}, u32[]{:S(2)}) %collective-permute-start.2) | collective-permute-done | bytes 589856 | tf_op jit(solution)/shard_map/ppermute | solution.py:42
  25.6 3.8 %collective-permute-start.5 = (bf16[128,3840]{1,0:T(8,128)(2,1)}, bf16[128,3840]{1,0:T(8,128)(2,1)}, u32[]{:S(2)}, u32[]{:S(2)}) collective-permute-start(bf16[128,3840]{1,0:T(8,128)(2,1)} %get-tuple-element.65), channel_id=1, source_target_pairs={{0,224},{32,0},{64,32},{96,64},{128,96},{160,128},{192,160},{224,1... | collective-permute-start | bytes 2949128 | tf_op jit(solution)/shard_map/ppermute | solution.py:42
  31.4 3.0 %collective-permute-start.7 = (bf16[8,144,128]{2,1,0:T(8,128)(2,1)S(1)}, bf16[8,144,128]{2,1,0:T(8,128)(2,1)S(1)}, u32[]{:S(2)}, u32[]{:S(2)}) collective-permute-start(bf16[8,144,128]{2,1,0:T(8,128)(2,1)S(1)} %get-tuple-element.68), channel_id=1, source_target_pairs={{0,2},{2,0},{1,3},{3,1},{4,6},{6,4},{5,7},{7,5},{8,10},{10,8},{9,1... | collective-permute-start | bytes 884744 | tf_op jit(solution)/shard_map/ppermute | solution.py:42
  34.4 7.2 %collective-permute-done.6.refs_4_ = bf16[256,768]{1,0:T(8,128)(2,1)S(1)} collective-permute-done((bf16[256,768]{1,0:T(8,128)(2,1)S(1)}, bf16[256,768]{1,0:T(8,128)(2,1)S(1)}, u32[]{:S(2)}, u32[]{:S(2)}) %collective-permute-start.6) | collective-permute-done | bytes 393248 | tf_op jit(solution)/shard_map/ppermute | solution.py:42
  41.6 8.4 %collective-permute-done.7 = bf16[8,144,128]{2,1,0:T(8,128)(2,1)S(1)} collective-permute-done((bf16[8,144,128]{2,1,0:T(8,128)(2,1)S(1)}, bf16[8,144,128]{2,1,0:T(8,128)(2,1)S(1)}, u32[]{:S(2)}, u32[]{:S(2)}) %collective-permute-start.7) | collective-permute-done | bytes 294944 | tf_op jit(solution)/shard_map/ppermute | solution.py:42
  57.0 1.7 %collective-permute-start.12 = (bf16[2,8,144,128]{3,2,1,0:T(8,128)(2,1)S(1)}, bf16[2,8,144,128]{3,2,1,0:T(8,128)(2,1)S(1)}, u32[]{:S(2)}, u32[]{:S(2)}) collective-permute-start(bf16[2,8,144,128]{3,2,1,0:T(8,128)(2,1)S(1)} %pad_maximum_fusion.3.xp), channel_id=1, source_target_pairs={{0,12},{4,0},{8,4},{12,8},{1,13},{5,1},{9,5},{13,9},{2,14},{6,2},{... | collective-permute-start | bytes 1769480 | tf_op jit(solution)/shard_map/ppermute | solution.py:42
  58.8 4.0 %collective-permute-done.10.refs_7_ = bf16[256,768]{1,0:T(8,128)(2,1)S(1)} collective-permute-done((bf16[256,768]{1,0:T(8,128)(2,1)S(1)}, bf16[256,768]{1,0:T(8,128)(2,1)S(1)}, u32[]{:S(2)}, u32[]{:S(2)}) %collective-permute-start.10) | collective-permute-done | bytes 393248 | tf_op jit(solution)/shard_map/ppermute | solution.py:42
  62.7 8.3 %collective-permute-done.11.f = bf16[2,8,144,128]{3,2,1,0:T(8,128)(2,1)S(1)} collective-permute-done((bf16[2,8,144,128]{3,2,1,0:T(8,128)(2,1)S(1)}, bf16[2,8,144,128]{3,2,1,0:T(8,128)(2,1)S(1)}, u32[]{:S(2)}, u32[]{:S(2)}) %collective-permute-start.11) | collective-permute-done | bytes 589856 | tf_op jit(solution)/shard_map/ppermute | solution.py:42
  71.1 5.8 %collective-permute-done.8.refs_8_ = bf16[128,3840]{1,0:T(8,128)(2,1)S(1)} collective-permute-done((bf16[128,3840]{1,0:T(8,128)(2,1)}, bf16[128,3840]{1,0:T(8,128)(2,1)S(1)}, u32[]{:S(2)}, u32[]{:S(2)}) %collective-permute-start.8) | collective-permute-done | bytes 983072 | tf_op jit(solution)/shard_map/ppermute | solution.py:42
  77.8 2.2 %collective-permute-start.15 = (bf16[128,2816]{1,0:T(8,128)(2,1)S(1)}, bf16[128,2816]{1,0:T(8,128)(2,1)S(1)}, u32[]{:S(2)}, u32[]{:S(2)}) collective-permute-start(bf16[128,2816]{1,0:T(8,128)(2,1)S(1)} %slice.52), channel_id=1, source_target_pairs={{0,224},{32,0},{64,32},{96,64},{128,96},{160,128},{192,160},{224,1... | collective-permute-start | bytes 2162696 | tf_op jit(solution)/shard_map/ppermute | solution.py:42
  80.0 1.7 %collective-permute-start.17 = (bf16[8,144,128]{2,1,0:T(8,128)(2,1)S(1)}, bf16[8,144,128]{2,1,0:T(8,128)(2,1)}, u32[]{:S(2)}, u32[]{:S(2)}) collective-permute-start(bf16[8,144,128]{2,1,0:T(8,128)(2,1)S(1)} %slice_bitcast_fusion.1), channel_id=1, source_target_pairs={{0,4},{4,8},{8,12},{12,0},{1,5},{5,9},{9,13},{13,1},{2,6},{6,10},{... | collective-permute-start | bytes 884744 | tf_op jit(solution)/shard_map/ppermute | solution.py:42
  81.8 1.8 %collective-permute-start.18 = (bf16[8,144,128]{2,1,0:T(8,128)(2,1)S(1)}, bf16[8,144,128]{2,1,0:T(8,128)(2,1)}, u32[]{:S(2)}, u32[]{:S(2)}) collective-permute-start(bf16[8,144,128]{2,1,0:T(8,128)(2,1)S(1)} %slice_bitcast_fusion), channel_id=1, source_target_pairs={{0,12},{4,0},{8,4},{12,8},{1,13},{5,1},{9,5},{13,9},{2,14},{6,2},{... | collective-permute-start | bytes 884744 | tf_op jit(solution)/shard_map/ppermute | solution.py:42
  83.9 4.8 %collective-permute-done.17.fa = bf16[8,144,128]{2,1,0:T(8,128)(2,1)} collective-permute-done((bf16[8,144,128]{2,1,0:T(8,128)(2,1)S(1)}, bf16[8,144,128]{2,1,0:T(8,128)(2,1)}, u32[]{:S(2)}, u32[]{:S(2)}) %collective-permute-start.17) | collective-permute-done | bytes 294944 | tf_op jit(solution)/shard_map/ppermute | solution.py:42
  90.4 10.0 %collective-permute-done.16.refs_10_ = bf16[256,768]{1,0:T(8,128)(2,1)S(1)} collective-permute-done((bf16[256,768]{1,0:T(8,128)(2,1)S(1)}, bf16[256,768]{1,0:T(8,128)(2,1)S(1)}, u32[]{:S(2)}, u32[]{:S(2)}) %collective-permute-start.16) | collective-permute-done | bytes 393248 | tf_op jit(solution)/shard_map/ppermute | solution.py:42
  107.9 5.3 %features.1.lhs_hbm = bf16[1152,2048]{1,0:T(8,128)(2,1)} custom-call(s32[5]{0:T(128)S(1)} %stack.32.pos, bf16[2,8,144,128]{3,2,1,0:T(8,128)(2,1)S(1)} %pad_maximum_fusion.3.xp, bf16[2,8,144,128]{3,2,1,0:T(8,128)(2,1)S(1)} %collective-permute-done.11.f, bf16[2,8,144,128]{3,2,1,0:T(8,128)(2,1)S(1)} %collective-permute-done.12.b, ...), custom_call_target="tpu_custom_call" | custom-call | bytes 9437184 | tf_op jit(solution)/shard_map/features/pallas_call | solution.py:68
  113.7 18.3 %product.1 = (f32[1152,2304]{1,0:T(8,128)}, f32[16,9,128]{2,1,0:T(8,128)}, f32[18,128]{1,0:T(8,128)S(1)}) custom-call(s32[5]{0:T(128)S(1)} %stack.32.pos, bf16[1152,2048]{1,0:T(8,128)(2,1)} %features.1.lhs_hbm, bf16[128,2304]{1,0:T(8,128)(2,1)S(1)} %fusion.5.refs_0_, bf16[128,2304]{1,0:T(8,128)(2,1)S(1)} %copy-done.1, ...), custom_call_target="tpu_custom_call" | custom-call | flops 10871635968 | bytes 20054016 | tf_op jit(solution)/shard_map/product/pallas_call | solution.py:254
  132.0 3.5 %all-to-all-start.1 = ((f32[16,9,128]{2,1,0:T(8,128)}), f32[16,9,128]{2,1,0:T(8,128)S(1)}, u32[]{:S(2)}, u32[]{:S(2)}) async-start(f32[16,9,128]{2,1,0:T(8,128)} %get-tuple-element.54), calls=%async_computation.1 | async-start | bytes 262144 | tf_op jit(solution)/shard_map/all_to_all | solution.py:328
  135.7 7.9 %all-to-all-done.1.got = f32[16,9,128]{2,1,0:T(8,128)S(1)} async-done(((f32[16,9,128]{2,1,0:T(8,128)}), f32[16,9,128]{2,1,0:T(8,128)S(1)}, u32[]{:S(2)}, u32[]{:S(2)}) %all-to-all-start.1) | async-done | bytes 73760 | tf_op jit(solution)/shard_map/all_to_all | solution.py:328
  144.3 5.9 %all-to-all-start.2 = ((f32[16,24,128]{2,1,0:T(8,128)}), f32[16,24,128]{2,1,0:T(8,128)S(1)}, u32[]{:S(2)}, u32[]{:S(2)}) async-start(f32[16,24,128]{2,1,0:T(8,128)} %get-tuple-element.56), calls=%async_computation.2 | async-start | bytes 393216 | tf_op jit(solution)/shard_map/all_to_all | solution.py:328
  150.9 10.4 %all-to-all-done.2.got = f32[16,24,128]{2,1,0:T(8,128)S(1)} async-done(((f32[16,24,128]{2,1,0:T(8,128)}), f32[16,24,128]{2,1,0:T(8,128)S(1)}, u32[]{:S(2)}, u32[]{:S(2)}) %all-to-all-start.2) | async-done | bytes 196640 | tf_op jit(solution)/shard_map/all_to_all | solution.py:328
  161.4 7.0 %update.1 = (bf16[1152,2304]{1,0:T(8,128)(2,1)}, f32[18,128]{1,0:T(8,128)}) custom-call(f32[16,24,128]{2,1,0:T(8,128)S(1)} %all-to-all-done.2.got, f32[9,128]{1,0:T(8,128)S(1)} %get-tuple-element.57.row_new, f32[18,128]{1,0:T(8,128)S(1)} %bitcast.17, f32[1152,2304]{1,0:T(8,128)} %get-tuple-element.58.grad), custom_call_target="tpu_custom_call" | custom-call | tf_op jit(solution)/shard_map/update/pallas_call | solution.py:349
  (105 shorter events, 27.1 us)
Async XLA Ops:
  2.2 19.0 %collective-permute-start.1 = (bf16[128,2304]{1,0:T(8,128)(2,1)S(1)}, bf16[128,2304]{1,0:T(8,128)(2,1)S(1)}, u32[]{:S(2)}, u32[]{:S(2)}) collective-permute-start(bf16[128,2304]{1,0:T(8,128)(2,1)S(1)} %fusion.5.refs_0_), channel_id=1, source_target_pairs={{0,32},{32,64},{64,96},{96,128},{128,160},{160,192},{192,224},{224... | collective-permute-start | bytes 1769480 | tf_op jit(solution)/shard_map/ppermute | solution.py:42
  2.4 21.6 %collective-permute-start.2 = (bf16[128,2304]{1,0:T(8,128)(2,1)S(1)}, bf16[128,2304]{1,0:T(8,128)(2,1)S(1)}, u32[]{:S(2)}, u32[]{:S(2)}) collective-permute-start(bf16[128,2304]{1,0:T(8,128)(2,1)S(1)} %fusion.5.refs_0_), channel_id=1, source_target_pairs={{0,224},{32,0},{64,32},{96,64},{128,96},{160,128},{192,160},{224,1... | collective-permute-start | bytes 1769480 | tf_op jit(solution)/shard_map/ppermute | solution.py:42
  6.4 17.6 %collective-permute-start.3 = (bf16[128,2304]{1,0:T(8,128)(2,1)S(1)}, bf16[128,2304]{1,0:T(8,128)(2,1)S(1)}, u32[]{:S(2)}, u32[]{:S(2)}) collective-permute-start(bf16[128,2304]{1,0:T(8,128)(2,1)S(1)} %fusion.5.refs_0_), channel_id=1, source_target_pairs={{0,16},{16,0},{1,17},{17,1},{2,18},{18,2},{3,19},{19,3},{4,20},{20... | collective-permute-start | bytes 1769480 | tf_op jit(solution)/shard_map/ppermute | solution.py:42
  8.9 20.5 %all-to-all-start = ((bf16[16,72,128]{2,1,0:T(8,128)(2,1)}), bf16[16,72,128]{2,1,0:T(8,128)(2,1)S(1)}, u32[]{:S(2)}, u32[]{:S(2)}) async-start(bf16[16,72,128]{2,1,0:T(8,128)(2,1)} %bitcast.6), calls=%async_computation | async-start | bytes 589824 | tf_op jit(solution)/shard_map/all_to_all | solution.py:109
  25.6 24.4 %collective-permute-start.4 = (bf16[128,3840]{1,0:T(8,128)(2,1)}, bf16[128,3840]{1,0:T(8,128)(2,1)}, u32[]{:S(2)}, u32[]{:S(2)}) collective-permute-start(bf16[128,3840]{1,0:T(8,128)(2,1)} %get-tuple-element.66), channel_id=1, source_target_pairs={{0,32},{32,64},{64,96},{96,128},{128,160},{160,192},{192,224},{224... | collective-permute-start | bytes 2949128 | tf_op jit(solution)/shard_map/ppermute | solution.py:42
  25.6 24.4 %collective-permute-start.5 = (bf16[128,3840]{1,0:T(8,128)(2,1)}, bf16[128,3840]{1,0:T(8,128)(2,1)}, u32[]{:S(2)}, u32[]{:S(2)}) collective-permute-start(bf16[128,3840]{1,0:T(8,128)(2,1)} %get-tuple-element.65), channel_id=1, source_target_pairs={{0,224},{32,0},{64,32},{96,64},{128,96},{160,128},{192,160},{224,1... | collective-permute-start | bytes 2949128 | tf_op jit(solution)/shard_map/ppermute | solution.py:42
  29.6 12.0 %collective-permute-start.6 = (bf16[256,768]{1,0:T(8,128)(2,1)S(1)}, bf16[256,768]{1,0:T(8,128)(2,1)S(1)}, u32[]{:S(2)}, u32[]{:S(2)}) collective-permute-start(bf16[256,768]{1,0:T(8,128)(2,1)S(1)} %pad_maximum_fusion.4), channel_id=1, source_target_pairs={{0,16},{16,0},{1,17},{17,1},{2,18},{18,2},{3,19},{19,3},{4,20},{20... | collective-permute-start | bytes 1179656 | tf_op jit(solution)/shard_map/ppermute | solution.py:42
  31.4 18.6 %collective-permute-start.7 = (bf16[8,144,128]{2,1,0:T(8,128)(2,1)S(1)}, bf16[8,144,128]{2,1,0:T(8,128)(2,1)S(1)}, u32[]{:S(2)}, u32[]{:S(2)}) collective-permute-start(bf16[8,144,128]{2,1,0:T(8,128)(2,1)S(1)} %get-tuple-element.68), channel_id=1, source_target_pairs={{0,2},{2,0},{1,3},{3,1},{4,6},{6,4},{5,7},{7,5},{8,10},{10,8},{9,1... | collective-permute-start | bytes 884744 | tf_op jit(solution)/shard_map/ppermute | solution.py:42
  51.9 10.8 %collective-permute-start.10 = (bf16[256,768]{1,0:T(8,128)(2,1)S(1)}, bf16[256,768]{1,0:T(8,128)(2,1)S(1)}, u32[]{:S(2)}, u32[]{:S(2)}) collective-permute-start(bf16[256,768]{1,0:T(8,128)(2,1)S(1)} %pad_maximum_fusion.5), channel_id=1, source_target_pairs={{0,16},{16,0},{1,17},{17,1},{2,18},{18,2},{3,19},{19,3},{4,20},{20... | collective-permute-start | bytes 1179656 | tf_op jit(solution)/shard_map/ppermute | solution.py:42
  52.1 24.7 %collective-permute-start.8 = (bf16[128,3840]{1,0:T(8,128)(2,1)}, bf16[128,3840]{1,0:T(8,128)(2,1)S(1)}, u32[]{:S(2)}, u32[]{:S(2)}) collective-permute-start(bf16[128,3840]{1,0:T(8,128)(2,1)} %collective-permute-done.4.refs_5_), channel_id=1, source_target_pairs={{0,32},{32,64},{64,96},{96,128},{128,160},{160,192},{192,224},{224... | collective-permute-start | bytes 2949128 | tf_op jit(solution)/shard_map/ppermute | solution.py:42
  53.7 23.1 %collective-permute-start.9 = (bf16[128,3840]{1,0:T(8,128)(2,1)}, bf16[128,3840]{1,0:T(8,128)(2,1)S(1)}, u32[]{:S(2)}, u32[]{:S(2)}) collective-permute-start(bf16[128,3840]{1,0:T(8,128)(2,1)} %collective-permute-done.5.refs_6_), channel_id=1, source_target_pairs={{0,224},{32,0},{64,32},{96,64},{128,96},{160,128},{192,160},{224,1... | collective-permute-start | bytes 2949128 | tf_op jit(solution)/shard_map/ppermute | solution.py:42
  55.4 15.6 %collective-permute-start.11 = (bf16[2,8,144,128]{3,2,1,0:T(8,128)(2,1)S(1)}, bf16[2,8,144,128]{3,2,1,0:T(8,128)(2,1)S(1)}, u32[]{:S(2)}, u32[]{:S(2)}) collective-permute-start(bf16[2,8,144,128]{3,2,1,0:T(8,128)(2,1)S(1)} %pad_maximum_fusion.3.xp), channel_id=1, source_target_pairs={{0,4},{4,8},{8,12},{12,0},{1,5},{5,9},{9,13},{13,1},{2,6},{6,10},{... | collective-permute-start | bytes 1769480 | tf_op jit(solution)/shard_map/ppermute | solution.py:42
  57.0 14.1 %collective-permute-start.12 = (bf16[2,8,144,128]{3,2,1,0:T(8,128)(2,1)S(1)}, bf16[2,8,144,128]{3,2,1,0:T(8,128)(2,1)S(1)}, u32[]{:S(2)}, u32[]{:S(2)}) collective-permute-start(bf16[2,8,144,128]{3,2,1,0:T(8,128)(2,1)S(1)} %pad_maximum_fusion.3.xp), channel_id=1, source_target_pairs={{0,12},{4,0},{8,4},{12,8},{1,13},{5,1},{9,5},{13,9},{2,14},{6,2},{... | collective-permute-start | bytes 1769480 | tf_op jit(solution)/shard_map/ppermute | solution.py:42
  62.7 8.3 %collective-permute-start.13 = (bf16[2,8,144,128]{3,2,1,0:T(8,128)(2,1)S(1)}, bf16[2,8,144,128]{3,2,1,0:T(8,128)(2,1)S(1)}, u32[]{:S(2)}, u32[]{:S(2)}) collective-permute-start(bf16[2,8,144,128]{3,2,1,0:T(8,128)(2,1)S(1)} %pad_maximum_fusion.3.xp), channel_id=1, source_target_pairs={{0,1},{1,0},{2,3},{3,2},{4,5},{5,4},{6,7},{7,6},{8,9},{9,8},{10,11... | collective-permute-start | bytes 1769480 | tf_op jit(solution)/shard_map/ppermute | solution.py:42
  77.8 23.3 %collective-permute-start.15 = (bf16[128,2816]{1,0:T(8,128)(2,1)S(1)}, bf16[128,2816]{1,0:T(8,128)(2,1)S(1)}, u32[]{:S(2)}, u32[]{:S(2)}) collective-permute-start(bf16[128,2816]{1,0:T(8,128)(2,1)S(1)} %slice.52), channel_id=1, source_target_pairs={{0,224},{32,0},{64,32},{96,64},{128,96},{160,128},{192,160},{224,1... | collective-permute-start | bytes 2162696 | tf_op jit(solution)/shard_map/ppermute | solution.py:42
  80.0 8.7 %collective-permute-start.17 = (bf16[8,144,128]{2,1,0:T(8,128)(2,1)S(1)}, bf16[8,144,128]{2,1,0:T(8,128)(2,1)}, u32[]{:S(2)}, u32[]{:S(2)}) collective-permute-start(bf16[8,144,128]{2,1,0:T(8,128)(2,1)S(1)} %slice_bitcast_fusion.1), channel_id=1, source_target_pairs={{0,4},{4,8},{8,12},{12,0},{1,5},{5,9},{9,13},{13,1},{2,6},{6,10},{... | collective-permute-start | bytes 884744 | tf_op jit(solution)/shard_map/ppermute | solution.py:42
  83.7 17.5 %collective-permute-start.14 = (bf16[128,2560]{1,0:T(8,128)(2,1)S(1)}, bf16[128,2560]{1,0:T(8,128)(2,1)S(1)}, u32[]{:S(2)}, u32[]{:S(2)}) collective-permute-start(bf16[128,2560]{1,0:T(8,128)(2,1)S(1)} %pad_maximum_fusion.2), channel_id=1, source_target_pairs={{0,32},{32,64},{64,96},{96,128},{128,160},{160,192},{192,224},{224... | collective-permute-start | bytes 1966088 | tf_op jit(solution)/shard_map/ppermute | solution.py:42
  83.8 17.4 %collective-permute-start.19 = (bf16[2,8,144,128]{3,2,1,0:T(8,128)(2,1)S(1)}, bf16[2,8,144,128]{3,2,1,0:T(8,128)(2,1)S(1)}, u32[]{:S(2)}, u32[]{:S(2)}) collective-permute-start(bf16[2,8,144,128]{3,2,1,0:T(8,128)(2,1)S(1)} %collective-permute-done.11.f), channel_id=1, source_target_pairs={{0,1},{1,0},{2,3},{3,2},{4,5},{5,4},{6,7},{7,6},{8,9},{9,8},{10,11... | collective-permute-start | bytes 1769480 | tf_op jit(solution)/shard_map/ppermute | solution.py:42
  88.7 12.4 %collective-permute-start.20 = (bf16[2,8,144,128]{3,2,1,0:T(8,128)(2,1)S(1)}, bf16[2,8,144,128]{3,2,1,0:T(8,128)(2,1)S(1)}, u32[]{:S(2)}, u32[]{:S(2)}) collective-permute-start(bf16[2,8,144,128]{3,2,1,0:T(8,128)(2,1)S(1)} %collective-permute-done.12.b), channel_id=1, source_target_pairs={{0,1},{1,0},{2,3},{3,2},{4,5},{5,4},{6,7},{7,6},{8,9},{9,8},{10,11... | collective-permute-start | bytes 1769480 | tf_op jit(solution)/shard_map/ppermute | solution.py:42
  88.8 11.6 %collective-permute-start.16 = (bf16[256,768]{1,0:T(8,128)(2,1)S(1)}, bf16[256,768]{1,0:T(8,128)(2,1)S(1)}, u32[]{:S(2)}, u32[]{:S(2)}) collective-permute-start(bf16[256,768]{1,0:T(8,128)(2,1)S(1)} %pad_maximum_fusion.6), channel_id=1, source_target_pairs={{0,16},{16,0},{1,17},{17,1},{2,18},{18,2},{3,19},{19,3},{4,20},{20... | collective-permute-start | bytes 1179656 | tf_op jit(solution)/shard_map/ppermute | solution.py:42
  103.6 9.6 %collective-permute-start.23 = (bf16[128,768]{1,0:T(8,128)(2,1)}, bf16[128,768]{1,0:T(8,128)(2,1)}, u32[]{:S(2)}, u32[]{:S(2)}) collective-permute-start(bf16[128,768]{1,0:T(8,128)(2,1)} %get-tuple-element.62), channel_id=1, source_target_pairs={{0,16},{16,0},{1,17},{17,1},{2,18},{18,2},{3,19},{19,3},{4,20},{20... | collective-permute-start | bytes 589832 | tf_op jit(solution)/shard_map/ppermute | solution.py:42
  105.0 8.2 %collective-permute-start.25 = (bf16[128,768]{1,0:T(8,128)(2,1)}, bf16[128,768]{1,0:T(8,128)(2,1)}, u32[]{:S(2)}, u32[]{:S(2)}) collective-permute-start(bf16[128,768]{1,0:T(8,128)(2,1)} %get-tuple-element.61), channel_id=1, source_target_pairs={{0,224},{32,0},{64,32},{96,64},{128,96},{160,128},{192,160},{224,1... | collective-permute-start | bytes 589832 | tf_op jit(solution)/shard_map/ppermute | solution.py:42
  132.0 11.5 %all-to-all-start.1 = ((f32[16,9,128]{2,1,0:T(8,128)}), f32[16,9,128]{2,1,0:T(8,128)S(1)}, u32[]{:S(2)}, u32[]{:S(2)}) async-start(f32[16,9,128]{2,1,0:T(8,128)} %get-tuple-element.54), calls=%async_computation.1 | async-start | bytes 262144 | tf_op jit(solution)/shard_map/all_to_all | solution.py:328
  144.3 17.0 %all-to-all-start.2 = ((f32[16,24,128]{2,1,0:T(8,128)}), f32[16,24,128]{2,1,0:T(8,128)S(1)}, u32[]{:S(2)}, u32[]{:S(2)}) async-start(f32[16,24,128]{2,1,0:T(8,128)} %get-tuple-element.56), calls=%async_computation.2 | async-start | bytes 393216 | tf_op jit(solution)/shard_map/all_to_all | solution.py:328
  (26 other events, 199.1 us)

commit v3 on v2

v3 whole, which is shorter than its diff:
```python
import functools

import jax
import jax.numpy as jnp
import numpy as np
from jax import lax
from jax.experimental import pallas as pl
from jax.experimental.pallas import tpu as pltpu
from jax.sharding import Mesh, PartitionSpec as P

D = 18432

decay = 1.0 - 2.0 ** (-0.8)
tiny = 1e-30

DP = ("z", "yl")
MP = ("x", "yh", "core")

TOK = 128
HID = 2304
WID = 72
OWN = 1152
ALL_TOK = 2048
FFW = 36864
CB = 256
BLOCKS = HID // CB
A_BLOCKS = 5
A_COLS = A_BLOCKS * CB
SPLIT = 4 * CB
A_UP = 3 * CB
EARLY = [(0, 0), (0, 1), (7, 0), (1, 0), (7, 1), (1, 1), (6, 0), (2, 0), (6, 1), (2, 1), (5, 0), (3, 0)]
LATE = [(5, 1), (3, 1), (4, 0), (4, 1)]
EARLY_TOK = len(EARLY) * TOK
LATE_TOK = len(LATE) * TOK
PLACES = np.array(
    [(EARLY + LATE).index((dz, dy)) for dz in range(8) for dy in range(2)], np.int32
)
MIB = 1024 * 1024
AHEAD = 3
LIMIT = 50 * MIB

ANY = pl.BlockSpec(memory_space=pl.ANY)
VMEM = pl.BlockSpec(memory_space=pltpu.VMEM)
SMEM = pl.BlockSpec(memory_space=pltpu.SMEM)


def ring(n, s):
    return [(i, (i + s) % n) for i in range(n)]


def send(v, axis, n, s):
    return lax.ppermute(v, axis, ring(n, s))


def tie(*v):
    return lax.optimization_barrier(v)


def up_z(v):
    return send(v, "z", 8, 1)


def down_z(v):
    return send(v, "z", 8, -1)


def other(v, axis):
    return send(v, axis, 2, 1)


def exchange(hidden, grad_out, pos):
    core = pos[4]

    def cross(*parts):
        return other(jnp.concatenate(parts, 0), "yl")

    def cut(v, first, last):
        return lax.slice_in_dim(v, first, last, axis=1)

    hidden, grad_out = tie(hidden, grad_out)
    u1, d1, near = up_z(hidden), down_z(hidden), other(hidden, "yl")
    turned = grad_out.T.reshape(16, WID, TOK)
    q = lax.all_to_all(turned, DP, 0, 0, tiled=True)
    u1, d1, near, q = tie(u1, d1, near, q)
    side = cut(near, 0, A_COLS)
    u2 = up_z(jnp.concatenate([u1, side], 1))
    d2 = down_z(jnp.concatenate([d1, side], 1))
    y1 = cross(cut(u1, A_COLS, HID), cut(d1, A_COLS, HID))
    keep = lax.dynamic_slice_in_dim(q, 8 * core, 8, 0)
    give = lax.dynamic_slice_in_dim(q, 8 - 8 * core, 8, 0)
    got = other(give, "core")
    first = jnp.where(core == 0, keep, got)
    second = jnp.where(core == 0, got, keep)
    half = jnp.concatenate([first, second], 1)
    far = other(half, "yh")
    f0, b0 = send(half, "x", 4, 1), send(half, "x", 4, -1)
    u2, d2, y1, far, f0, b0 = tie(u2, d2, y1, far, f0, b0)
    u3, d3 = up_z(u2), down_z(d2)
    y2 = cross(cut(u2, A_COLS, HID), cut(d2, A_COLS, HID))
    f1, b1 = send(far, "x", 4, 1), send(far, "x", 4, -1)
    o0 = send(f0, "x", 4, 1)
    o1 = send(b1, "x", 4, -1)
    mine = [half, f0, b0, o0, far, f1, b1, o1]
    theirs = [other(v, "core") for v in mine]
    u3, d3, y2, f1, o0, o1 = tie(u3, d3, y2, f1, o0, o1)
    u4 = up_z(jnp.concatenate([cut(u3, 0, SPLIT), cut(u3, HID, HID + A_COLS)], 1))
    d4 = down_z(cut(d3, SPLIT, HID + A_COLS))
    y3 = cross(cut(u3, A_COLS, HID), cut(d3, A_COLS, HID))
    features = mine + theirs
    n, m, h, k = BLOCKS, A_BLOCKS, SPLIT // CB, A_UP // CB
    pieces = [
        (hidden, 0, 0, 0, 0, 0, n),
        (near, 0, 0, 0, 1, 0, n),
        (u1, 0, 0, 7, 0, 0, n),
        (d1, 0, 0, 1, 0, 0, n),
        (y1, 0, -A_COLS, 7, 1, m, n),
        (y1, TOK, -A_COLS, 1, 1, m, n),
        (u2, 0, 0, 6, 0, 0, n),
        (d2, 0, 0, 2, 0, 0, n),
        (u2, 0, HID, 7, 1, 0, m),
        (d2, 0, HID, 1, 1, 0, m),
        (y2, 0, -A_COLS, 6, 1, m, n),
        (y2, TOK, -A_COLS, 2, 1, m, n),
        (u3, 0, 0, 5, 0, 0, n),
        (d3, 0, 0, 3, 0, 0, n),
        (u3, 0, HID, 6, 1, 0, m),
        (d3, 0, HID, 2, 1, 0, m),
    ]
    early, lhs = early_product(features, pieces, pos)
    u4, d4, y3, early = tie(u4, d4, y3, early)
    u5 = up_z(cut(u4, SPLIT, SPLIT + A_UP))
    d5 = down_z(cut(d4, HID - SPLIT + A_UP, HID - SPLIT + A_COLS))
    y4 = cross(cut(d4, A_COLS - SPLIT, HID - SPLIT))
    pieces = [
        (y3, 0, -A_COLS, 5, 1, m, n),
        (y3, TOK, -A_COLS, 3, 1, m, n),
        (u4, 0, 0, 4, 0, 0, h),
        (d4, 0, -SPLIT, 4, 0, h, n),
        (u4, 0, SPLIT, 5, 1, 0, m),
        (d4, 0, HID - SPLIT, 3, 1, 0, m),
        (y4, 0, -A_COLS, 4, 1, m, n),
        (u5, 0, 0, 4, 1, 0, k),
        (d5, 0, -A_UP, 4, 1, k, m),
    ]
    return late_product(lhs, early, pieces, pos)


def loader(plan, order, arrays, hid, hsem, z, yl):
    edges = sorted({p[5] for p in plan} | {p[6] for p in plan})

    def issue(j, slot):
        for lo, hi in zip(edges[:-1], edges[1:]):

            @pl.when((j >= lo) & (j < hi))
            def _(lo=lo):
                for index, row, base, dz, dy, first, last in plan:
                    if not first <= lo < last:
                        continue
                    col = pl.multiple_of(j * CB + base, CB)
                    place = order.index((dz, dy)) * TOK
                    pltpu.make_async_copy(
                        arrays[index].at[pl.ds(row, TOK), pl.ds(col, CB)],
                        hid.at[slot, place : place + TOK, :],
                        hsem.at[slot],
                    ).start()

    return issue


def column_block(grad, j):
    return grad.at[:, pl.ds(pl.multiple_of(j * CB, CB), CB)]


def early_kernel(plan, pos, places, *refs):
    features = refs[:16]
    arrays = refs[16:-25]
    grad, lhs_late = refs[-25:-23]
    stages = refs[-23:-7]
    lhs, hid, outbuf, fsem, lsem, hsem, osem = refs[-7:]
    z, yl, x, yh, core = pos[0], pos[1], pos[2], pos[3], pos[4]
    issue = loader(plan, EARLY, arrays, hid, hsem, z, yl)
    for k in range(16):
        pltpu.make_async_copy(features[k], stages[k], fsem.at[k]).start()
    issue(jnp.int32(0), 0)
    for k in range(16):
        pltpu.make_async_copy(features[k], stages[k], fsem.at[k]).wait()
        half = core if k < 8 else 1 - core
        dx, dy = (0, 3, 1, 2)[k % 4], (k // 4) % 2
        row = (lax.rem(x + dx, 4) * 2 + lax.rem(yh + dy, 2)) * (2 * WID)
        row = pl.multiple_of(row, 16)
        for i in range(8):
            s = half * 8 + i
            dz = lax.rem(s // 2 + 8 - z, 8)
            dy = lax.rem(lax.rem(s, 2) + 2 - yl, 2)
            col = pl.multiple_of(places[dz * 2 + dy] * TOK, TOK)
            lhs[pl.ds(row, 2 * WID), pl.ds(col, TOK)] = stages[k][i]
    late_copy = pltpu.make_async_copy(lhs.at[:, EARLY_TOK:], lhs_late, lsem)
    late_copy.start()

    def step(j, carry):
        slot = lax.rem(j, 2)

        @pl.when(j + 1 < BLOCKS)
        def _():
            issue(j + 1, 1 - slot)

        pltpu.make_async_copy(hid.at[slot], hid.at[slot], hsem.at[slot]).wait()

        @pl.when(j >= 2)
        def _():
            pltpu.make_async_copy(
                outbuf.at[slot], column_block(grad, j - 2), osem.at[slot]
            ).wait()

        for r in range(0, OWN, 384):
            outbuf[slot, r : r + 384, :] = jnp.dot(
                lhs[r : r + 384, :EARLY_TOK], hid[slot], preferred_element_type=jnp.float32
            )
        pltpu.make_async_copy(outbuf.at[slot], column_block(grad, j), osem.at[slot]).start()
        return carry

    lax.fori_loop(0, BLOCKS, step, 0)
    late_copy.wait()
    for j in range(BLOCKS - 2, BLOCKS):
        pltpu.make_async_copy(
            outbuf.at[j % 2], grad.at[:, j * CB : (j + 1) * CB], osem.at[j % 2]
        ).wait()


def numbered(pieces):
    arrays = []
    plan = []
    for piece in pieces:
        index = [i for i, a in enumerate(arrays) if a is piece[0]]
        if not index:
            arrays.append(piece[0])
            index = [len(arrays) - 1]
        plan.append((index[0],) + piece[1:])
    return arrays, plan


def early_product(features, pieces, pos):
    arrays, plan = numbered(pieces)
    return pl.pallas_call(
        functools.partial(early_kernel, plan),
        out_shape=(
            jax.ShapeDtypeStruct((OWN, HID), jnp.float32),
            jax.ShapeDtypeStruct((OWN, LATE_TOK), jnp.bfloat16),
        ),
        in_specs=[SMEM, SMEM] + [ANY] * (16 + len(arrays)),
        out_specs=(ANY, ANY),
        scratch_shapes=[pltpu.VMEM(v.shape, jnp.bfloat16) for v in features]
        + [
            pltpu.VMEM((OWN, ALL_TOK), jnp.bfloat16),
            pltpu.VMEM((2, EARLY_TOK, CB), jnp.bfloat16),
            pltpu.VMEM((2, OWN, CB), jnp.float32),
            pltpu.SemaphoreType.DMA((16,)),
            pltpu.SemaphoreType.DMA,
            pltpu.SemaphoreType.DMA((2,)),
            pltpu.SemaphoreType.DMA((2,)),
        ],
        compiler_params=pltpu.CompilerParams(vmem_limit_bytes=LIMIT),
        cost_estimate=pl.CostEstimate(
            flops=2 * OWN * HID * EARLY_TOK,
            bytes_accessed=OWN * HID * 4 + EARLY_TOK * HID * 2 + OWN * ALL_TOK * 2,
            transcendentals=0,
        ),
        name="early",
    )(pos, jnp.asarray(PLACES), *features, *arrays)


def late_kernel(plan, count, pos, lhs_hbm, before, *refs):
    arrays = refs[:count]
    grad, rows_out, cols_out = refs[count : count + 3]
    lhs, hid, whole, rowacc, lsem, hsem, bsem, osem = refs[count + 3 :]
    z, yl = pos[0], pos[1]
    issue = loader(plan, LATE, arrays, hid, hsem, z, yl)

    def block(j):
        return whole.at[:, pl.ds(pl.multiple_of(j * CB, CB), CB)]

    pltpu.make_async_copy(lhs_hbm, lhs, lsem).start()

    def fetch(j):
        issue(j, j)
        pltpu.make_async_copy(column_block(before, j), block(j), bsem.at[j]).start()

    for j in range(AHEAD):
        fetch(jnp.int32(j))
    rowacc[...] = jnp.zeros_like(rowacc)
    pltpu.make_async_copy(lhs_hbm, lhs, lsem).wait()

    def step(j, carry):
        @pl.when(j + AHEAD < BLOCKS)
        def _():
            fetch(j + AHEAD)

        pltpu.make_async_copy(hid.at[j], hid.at[j], hsem.at[j]).wait()
        pltpu.make_async_copy(column_block(before, j), block(j), bsem.at[j]).wait()
        cols = pl.ds(pl.multiple_of(j * CB, CB), CB)
        col = jnp.zeros((8, CB), jnp.float32)
        for r in range(0, OWN, 384):
            g = (
                jnp.dot(lhs[r : r + 384, :], hid[j], preferred_element_type=jnp.float32)
                + whole[r : r + 384, cols]
            ) * (1.0 / ALL_TOK)
            whole[r : r + 384, cols] = g
            sq = g * g
            rowacc[r : r + 384, :] += sq[:, :128] + sq[:, 128:]
            col = col + jnp.sum(sq.reshape(48, 8, CB), axis=0)
        total = jnp.sum(col, axis=0, keepdims=True)
        cols_out[pl.ds(2 * j, 1), :] = total[:, :128]
        cols_out[pl.ds(2 * j + 1, 1), :] = total[:, 128:]
        pltpu.make_async_copy(block(j), column_block(grad, j), osem.at[j]).start()
        return carry

    lax.fori_loop(0, BLOCKS, step, 0)
    for i in range(9):
        part = rowacc[i * 128 : (i + 1) * 128, :]
        line = jnp.sum(part.T, axis=0, keepdims=True)
        for d in range(16):
            rows_out[d, i : i + 1, :] = line
    for j in range(BLOCKS):
        pltpu.make_async_copy(
            block(jnp.int32(j)), column_block(grad, jnp.int32(j)), osem.at[j]
        ).wait()


def late_product(lhs, early, pieces, pos):
    arrays, plan = numbered(pieces)
    return pl.pallas_call(
        functools.partial(late_kernel, plan, len(arrays)),
        out_shape=(
            jax.ShapeDtypeStruct((OWN, HID), jnp.float32),
            jax.ShapeDtypeStruct((16, 9, 128), jnp.float32),
            jax.ShapeDtypeStruct((18, 128), jnp.float32),
        ),
        in_specs=[SMEM] + [ANY] * (2 + len(arrays)),
        out_specs=(ANY, VMEM, VMEM),
        scratch_shapes=[
            pltpu.VMEM((OWN, LATE_TOK), jnp.bfloat16),
            pltpu.VMEM((BLOCKS, LATE_TOK, CB), jnp.bfloat16),
            pltpu.VMEM((OWN, HID), jnp.float32),
            pltpu.VMEM((OWN, 128), jnp.float32),
            pltpu.SemaphoreType.DMA,
            pltpu.SemaphoreType.DMA((BLOCKS,)),
            pltpu.SemaphoreType.DMA((BLOCKS,)),
            pltpu.SemaphoreType.DMA((BLOCKS,)),
        ],
        compiler_params=pltpu.CompilerParams(vmem_limit_bytes=LIMIT),
        cost_estimate=pl.CostEstimate(
            flops=2 * OWN * HID * LATE_TOK,
            bytes_accessed=OWN * HID * 8 + LATE_TOK * HID * 2,
            transcendentals=0,
        ),
        name="late",
    )(pos, lhs, early, *arrays)


def middle_kernel(got, row_state, cols, row_new, payload):
    row_sum = jnp.sum(got[...], axis=0)
    new = decay * row_state[...] + (1.0 - decay) * (row_sum / FFW + tiny)
    row_new[...] = new
    total = jnp.sum(jnp.sum(new, axis=0, keepdims=True), axis=1, keepdims=True)
    for d in range(16):
        payload[d, :18, :] = cols[...]
        payload[d, 18:, :] = jnp.broadcast_to(total, (6, 128))


STRIPES = 9


def update_kernel(got, row_new, col_state, grad, out, col_new, colf, gbuf, obuf, rsem, wsem):
    def read(i):
        rows = pl.ds(i * 128, 128)
        return pltpu.make_async_copy(grad.at[rows, :], gbuf.at[rows, :], rsem.at[i])

    def write(i):
        rows = pl.ds(i * 128, 128)
        return pltpu.make_async_copy(obuf.at[rows, :], out.at[rows, :], wsem.at[i])

    for i in range(AHEAD):
        read(i).start()
    sums = jnp.sum(got[...], axis=0)
    new = decay * col_state[...] + (1.0 - decay) * (sums[:18, :] / D + tiny)
    col_new[...] = new
    inv = lax.rsqrt(new)
    for k in range(18):
        colf[:, k * 128 : (k + 1) * 128] = jnp.broadcast_to(inv[k : k + 1, :], (8, 128))
    scale = sums[18:19, :] / D
    rowf = lax.rsqrt(row_new[...]) * jnp.sqrt(scale)
    for i in range(STRIPES):
        if i + AHEAD < STRIPES:
            read(i + AHEAD).start()
        column = jnp.broadcast_to(rowf[i : i + 1, :], (128, 128)).T
        read(i).wait()
        for k in range(18):
            sl = slice(k * 128, (k + 1) * 128)
            obuf[i * 128 : (i + 1) * 128, sl] = (
                gbuf[i * 128 : (i + 1) * 128, sl] * (column * colf[0:1, sl])
            ).astype(jnp.bfloat16)
        write(i).start()
    for i in range(STRIPES):
        write(i).wait()


def spread(v, axes):
    return lax.all_to_all(v, axes, 0, 0, tiled=True)


def body(pre_act, grad_out, row_state, col_state):
    pos = jnp.stack([lax.axis_index(a) for a in ("z", "yl", "x", "yh", "core")]).astype(
        jnp.int32
    )
    hidden = jax.nn.gelu(pre_act.astype(jnp.float32)).astype(jnp.bfloat16)
    grad, rows, cols = exchange(hidden, grad_out, pos)
    row_new, payload = pl.pallas_call(
        middle_kernel,
        out_shape=(
            jax.ShapeDtypeStruct((9, 128), jnp.float32),
            jax.ShapeDtypeStruct((16, 24, 128), jnp.float32),
        ),
        in_specs=[VMEM] * 3,
        out_specs=(VMEM, VMEM),
        compiler_params=pltpu.CompilerParams(vmem_limit_bytes=4 * MIB),
        name="middle",
    )(spread(rows, MP), row_state.reshape(9, 128), cols)
    update, col_new = pl.pallas_call(
        update_kernel,
        out_shape=(
            jax.ShapeDtypeStruct((OWN, HID), jnp.bfloat16),
            jax.ShapeDtypeStruct((18, 128), jnp.float32),
        ),
        in_specs=[VMEM, VMEM, VMEM, ANY],
        out_specs=(ANY, VMEM),
        scratch_shapes=[
            pltpu.VMEM((8, HID), jnp.float32),
            pltpu.VMEM((OWN, HID), jnp.float32),
            pltpu.VMEM((OWN, HID), jnp.bfloat16),
            pltpu.SemaphoreType.DMA((STRIPES,)),
            pltpu.SemaphoreType.DMA((STRIPES,)),
        ],
        compiler_params=pltpu.CompilerParams(vmem_limit_bytes=LIMIT),
        name="update",
    )(spread(payload, DP), row_new, col_state.reshape(18, 128), grad)
    return (
        update.reshape(16, WID, HID),
        row_new.reshape(16, WID),
        col_new.reshape(HID),
    )


def solution(mesh):
    fine = Mesh(mesh.devices.reshape(8, 2, 4, 2, 2), ("z", "yl", "x", "yh", "core"))
    return jax.shard_map(
        body,
        mesh=fine,
        in_specs=(P(DP, MP), P(DP, MP), P(None, DP), P(MP)),
        out_specs=(P(None, DP, MP), P(None, DP), P(MP)),
        check_vma=False,
    )
```

time: 170 us -> 162 us (0.953)
  waiting for transfers between devices: 76.6 us -> 62 us
  starting transfers between devices: 47.8 us -> 51.1 us
  Pallas kernels: 31.5 us -> 34.3 us
    ppermute x26 -> x31, waiting for transfers between devices: 58.3 us -> 30.9 us  [send(): return lax.ppermute(v, axis, ring(n, s))]
    all_to_all x1, waiting for transfers between devices: 0.01 us -> 12.8 us  [exchange(): q = lax.all_to_all(turned, DP, 0, 0, tiled=True)]
    ppermute x26 -> x31, starting transfers between devices: 32.5 us -> 36.4 us  [send(): return lax.ppermute(v, axis, ring(n, s))]
    pallas_call x2, Pallas kernels: 23.6 us -> 26.3 us  [the longest x1 16 us: early_product(): pl.pallas_call(functools.partial(early_kernel, plan), out_shape=(jax.Shap...]
  transfers between devices with their start and end apart: 29 -> 34, of which waited for: 12 -> 13; matrix products, arithmetic and copies ran while one was open for 3% -> 4% of each run, Pallas kernels for 3% -> 10%
where the time goes in v3:
time: 162 us; the launch traced here: 159 us
  waiting for transfers between devices  62 us (38%)
  starting transfers between devices  51.1 us (32%)
  Pallas kernels  34.3 us (21%)
  local copies, waits for them, and re-layouts  8.23 us (5%)
  other arithmetic  2.62 us (2%)
    ppermute x31, starting transfers between devices, send(): return lax.ppermute(v, axis, ring(n, s))  36.4 us
    ppermute x31, waiting for transfers between devices, send(): return lax.ppermute(v, axis, ring(n, s))  30.9 us
    all_to_all x2, waiting for transfers between devices, spread(): return lax.all_to_all(v, axes, 0, 0, tiled=True)  18.3 us
    pallas_call x1, Pallas kernels, early_product(): pl.pallas_call(functools.partial(early_kernel, plan), out_shape=(jax.Shap...  16 us
    all_to_all x1, waiting for transfers between devices, exchange(): q = lax.all_to_all(turned, DP, 0, 0, tiled=True)  12.8 us
    pallas_call x1, Pallas kernels, late_product(): pl.pallas_call(functools.partial(late_kernel, plan, len(arrays)), out_sha...  10.4 us
    all_to_all x2, starting transfers between devices, spread(): return lax.all_to_all(v, axes, 0, 0, tiled=True)  8.87 us
    pallas_call x1, Pallas kernels, body(): pl.pallas_call(update_kernel, out_shape=(jax.ShapeDtypeStruct((OWN, HID),...  7.22 us
  transfers between devices with their start and end apart: 34, of which 13 were waited for; matrix products, arithmetic and copies ran while one was open for 4% of the time, Pallas kernels for 10%

profile of v3, /device:TPU:0, one launch (start us, length us, event | category | flops | bytes accessed | tf_op | source)
XLA Modules:
  0.0 159.5 jit_solution(5479735191773147587)
XLA Ops:
  2.4 4.0 %collective-permute-start.1 = (bf16[128,2304]{1,0:T(8,128)(2,1)S(1)}, bf16[128,2304]{1,0:T(8,128)(2,1)S(1)}, u32[]{:S(2)}, u32[]{:S(2)}) collective-permute-start(bf16[128,2304]{1,0:T(8,128)(2,1)S(1)} %fusion.5.refs_16_), channel_id=1, source_target_pairs={{0,224},{32,0},{64,32},{96,64},{128,96},{160,128},{192,160},{224,1... | collective-permute-start | bytes 1769480 | tf_op jit(solution)/shard_map/ppermute | solution.py:52
  8.9 5.9 %all-to-all-start = ((bf16[16,72,128]{2,1,0:T(8,128)(2,1)}), bf16[16,72,128]{2,1,0:T(8,128)(2,1)S(1)}, u32[]{:S(2)}, u32[]{:S(2)}) async-start(bf16[16,72,128]{2,1,0:T(8,128)(2,1)} %bitcast.6), calls=%async_computation | async-start | bytes 589824 | tf_op jit(solution)/shard_map/all_to_all | solution.py:83
  14.8 12.8 %all-to-all-done = bf16[16,72,128]{2,1,0:T(8,128)(2,1)S(1)} async-done(((bf16[16,72,128]{2,1,0:T(8,128)(2,1)}), bf16[16,72,128]{2,1,0:T(8,128)(2,1)S(1)}, u32[]{:S(2)}, u32[]{:S(2)}) %all-to-all-start) | async-done | bytes 294944 | tf_op jit(solution)/shard_map/all_to_all | solution.py:83
  28.8 3.6 %collective-permute-start.4 = (bf16[128,3584]{1,0:T(8,128)(2,1)S(1)}, bf16[128,3584]{1,0:T(8,128)(2,1)}, u32[]{:S(2)}, u32[]{:S(2)}) collective-permute-start(bf16[128,3584]{1,0:T(8,128)(2,1)S(1)} %get-tuple-element.64), channel_id=1, source_target_pairs={{0,32},{32,64},{64,96},{96,128},{128,160},{160,192},{192,224},{224... | collective-permute-start | bytes 2752520 | tf_op jit(solution)/shard_map/ppermute | solution.py:52
  32.5 3.0 %collective-permute-start.7 = (bf16[8,144,128]{2,1,0:T(8,128)(2,1)S(1)}, bf16[8,144,128]{2,1,0:T(8,128)(2,1)S(1)}, u32[]{:S(2)}, u32[]{:S(2)}) collective-permute-start(bf16[8,144,128]{2,1,0:T(8,128)(2,1)S(1)} %pad_maximum_fusion.6.refs_0_), channel_id=1, source_target_pairs={{0,2},{2,0},{1,3},{3,1},{4,6},{6,4},{5,7},{7,5},{8,10},{10,8},{9,1... | collective-permute-start | bytes 884744 | tf_op jit(solution)/shard_map/ppermute | solution.py:52
  37.2 6.8 %collective-permute-done.7.refs_4_ = bf16[8,144,128]{2,1,0:T(8,128)(2,1)S(1)} collective-permute-done((bf16[8,144,128]{2,1,0:T(8,128)(2,1)S(1)}, bf16[8,144,128]{2,1,0:T(8,128)(2,1)S(1)}, u32[]{:S(2)}, u32[]{:S(2)}) %collective-permute-start.7) | collective-permute-done | bytes 294944 | tf_op jit(solution)/shard_map/ppermute | solution.py:52
  44.0 2.8 %collective-permute-start.9 = (bf16[8,144,128]{2,1,0:T(8,128)(2,1)S(1)}, bf16[8,144,128]{2,1,0:T(8,128)(2,1)S(1)}, u32[]{:S(2)}, u32[]{:S(2)}) collective-permute-start(bf16[8,144,128]{2,1,0:T(8,128)(2,1)S(1)} %pad_maximum_fusion.6.refs_0_), channel_id=1, source_target_pairs={{0,12},{4,0},{8,4},{12,8},{1,13},{5,1},{9,5},{13,9},{2,14},{6,2},{... | collective-permute-start | bytes 884744 | tf_op jit(solution)/shard_map/ppermute | solution.py:52
  46.8 4.2 %collective-permute-done.9.refs_2_ = bf16[8,144,128]{2,1,0:T(8,128)(2,1)S(1)} collective-permute-done((bf16[8,144,128]{2,1,0:T(8,128)(2,1)S(1)}, bf16[8,144,128]{2,1,0:T(8,128)(2,1)S(1)}, u32[]{:S(2)}, u32[]{:S(2)}) %collective-permute-start.9) | collective-permute-done | bytes 294944 | tf_op jit(solution)/shard_map/ppermute | solution.py:52
  51.0 2.2 %collective-permute-done.6.refs_20_ = bf16[256,1024]{1,0:T(8,128)(2,1)S(1)} collective-permute-done((bf16[256,1024]{1,0:T(8,128)(2,1)S(1)}, bf16[256,1024]{1,0:T(8,128)(2,1)S(1)}, u32[]{:S(2)}, u32[]{:S(2)}) %collective-permute-start.6) | collective-permute-done | bytes 524320 | tf_op jit(solution)/shard_map/ppermute | solution.py:52
  55.0 2.4 %collective-permute-start.23 = (bf16[128,3584]{1,0:T(8,128)(2,1)}, bf16[128,3584]{1,0:T(8,128)(2,1)}, u32[]{:S(2)}, u32[]{:S(2)}) collective-permute-start(bf16[128,3584]{1,0:T(8,128)(2,1)} %collective-permute-done.5.refs_22_), channel_id=1, source_target_pairs={{0,224},{32,0},{64,32},{96,64},{128,96},{160,128},{192,160},{224,1... | collective-permute-start | bytes 2752520 | tf_op jit(solution)/shard_map/ppermute | solution.py:52
  59.4 2.8 %collective-permute-start.12 = (bf16[8,144,128]{2,1,0:T(8,128)(2,1)S(1)}, bf16[8,144,128]{2,1,0:T(8,128)(2,1)S(1)}, u32[]{:S(2)}, u32[]{:S(2)}) collective-permute-start(bf16[8,144,128]{2,1,0:T(8,128)(2,1)S(1)} %collective-permute-done.7.refs_4_), channel_id=1, source_target_pairs={{0,12},{4,0},{8,4},{12,8},{1,13},{5,1},{9,5},{13,9},{2,14},{6,2},{... | collective-permute-start | bytes 884744 | tf_op jit(solution)/shard_map/ppermute | solution.py:52
  64.0 2.6 %collective-permute-done.12.refs_6_ = bf16[8,144,128]{2,1,0:T(8,128)(2,1)S(1)} collective-permute-done((bf16[8,144,128]{2,1,0:T(8,128)(2,1)S(1)}, bf16[8,144,128]{2,1,0:T(8,128)(2,1)S(1)}, u32[]{:S(2)}, u32[]{:S(2)}) %collective-permute-start.12) | collective-permute-done | bytes 294944 | tf_op jit(solution)/shard_map/ppermute | solution.py:52
  67.9 4.2 %collective-permute-done.10.refs_3_ = bf16[8,144,128]{2,1,0:T(8,128)(2,1)S(1)} collective-permute-done((bf16[8,144,128]{2,1,0:T(8,128)(2,1)S(1)}, bf16[8,144,128]{2,1,0:T(8,128)(2,1)S(1)}, u32[]{:S(2)}, u32[]{:S(2)}) %collective-permute-start.10) | collective-permute-done | bytes 294944 | tf_op jit(solution)/shard_map/ppermute | solution.py:52
  72.1 4.3 %collective-permute-done.11.refs_5_ = bf16[8,144,128]{2,1,0:T(8,128)(2,1)S(1)} collective-permute-done((bf16[8,144,128]{2,1,0:T(8,128)(2,1)S(1)}, bf16[8,144,128]{2,1,0:T(8,128)(2,1)S(1)}, u32[]{:S(2)}, u32[]{:S(2)}) %collective-permute-start.11) | collective-permute-done | bytes 294944 | tf_op jit(solution)/shard_map/ppermute | solution.py:52
  84.9 1.8 %collective-permute-start.26 = (bf16[128,2560]{1,0:T(8,128)(2,1)S(1)}, bf16[128,2560]{1,0:T(8,128)(2,1)S(1)}, u32[]{:S(2)}, u32[]{:S(2)}) collective-permute-start(bf16[128,2560]{1,0:T(8,128)(2,1)S(1)} %slice.46), channel_id=1, source_target_pairs={{0,224},{32,0},{64,32},{96,64},{128,96},{160,128},{192,160},{224,1... | collective-permute-start | bytes 1966088 | tf_op jit(solution)/shard_map/ppermute | solution.py:52
  88.2 16.0 %early.1 = (f32[1152,2304]{1,0:T(8,128)}, bf16[1152,512]{1,0:T(8,128)(2,1)}) custom-call(s32[5]{0:T(128)S(1)} %stack.23.pos, s32[16]{0:T(128)S(1)} %copy-done.2, bf16[8,144,128]{2,1,0:T(8,128)(2,1)S(1)} %pad_maximum_fusion.6.refs_0_, bf16[8,144,128]{2,1,0:T(8,128)(2,1)S(1)} %collective-permute-done.8.refs_1_, ...), custom_call_target="tpu_custom_call" | custom-call | flops 8153726976 | bytes 22413312 | tf_op jit(solution)/shard_map/early/pallas_call | solution.py:244
  105.8 3.5 %collective-permute-start.30 = (bf16[128,512]{1,0:T(8,128)(2,1)S(1)}, bf16[128,512]{1,0:T(8,128)(2,1)S(1)}, u32[]{:S(2)}, u32[]{:S(2)}) collective-permute-start(bf16[128,512]{1,0:T(8,128)(2,1)S(1)} %slice.51), channel_id=1, source_target_pairs={{0,224},{32,0},{64,32},{96,64},{128,96},{160,128},{192,160},{224,1... | collective-permute-start | bytes 393224 | tf_op jit(solution)/shard_map/ppermute | solution.py:52
  109.3 2.5 %collective-permute-done.30.refs_5_ = bf16[128,512]{1,0:T(8,128)(2,1)S(1)} collective-permute-done((bf16[128,512]{1,0:T(8,128)(2,1)S(1)}, bf16[128,512]{1,0:T(8,128)(2,1)S(1)}, u32[]{:S(2)}, u32[]{:S(2)}) %collective-permute-start.30) | collective-permute-done | bytes 131104 | tf_op jit(solution)/shard_map/ppermute | solution.py:52
  113.0 10.4 %late.1 = (f32[1152,2304]{1,0:T(8,128)}, f32[16,9,128]{2,1,0:T(8,128)}, f32[18,128]{1,0:T(8,128)S(1)}) custom-call(s32[5]{0:T(128)S(1)} %stack.23.pos, bf16[1152,512]{1,0:T(8,128)(2,1)S(1)} %copy-done, f32[1152,2304]{1,0:T(8,128)} %get-tuple-element.48.before, bf16[256,1024]{1,0:T(8,128)(2,1)S(1)} %collective-permute-done.27.refs_0_, ...), custom_call_target="tpu_custom_call" | custom-call | flops 2717908992 | bytes 23592960 | tf_op jit(solution)/shard_map/late/pallas_call | solution.py:331
  123.3 4.9 %all-to-all-start.1 = ((f32[16,9,128]{2,1,0:T(8,128)}), f32[16,9,128]{2,1,0:T(8,128)S(1)}, u32[]{:S(2)}, u32[]{:S(2)}) async-start(f32[16,9,128]{2,1,0:T(8,128)} %get-tuple-element.52), calls=%async_computation.1 | async-start | bytes 262144 | tf_op jit(solution)/shard_map/all_to_all | solution.py:408
  128.4 7.9 %all-to-all-done.1.got = f32[16,9,128]{2,1,0:T(8,128)S(1)} async-done(((f32[16,9,128]{2,1,0:T(8,128)}), f32[16,9,128]{2,1,0:T(8,128)S(1)}, u32[]{:S(2)}, u32[]{:S(2)}) %all-to-all-start.1) | async-done | bytes 73760 | tf_op jit(solution)/shard_map/all_to_all | solution.py:408
  137.0 3.9 %all-to-all-start.2 = ((f32[16,24,128]{2,1,0:T(8,128)}), f32[16,24,128]{2,1,0:T(8,128)S(1)}, u32[]{:S(2)}, u32[]{:S(2)}) async-start(f32[16,24,128]{2,1,0:T(8,128)} %get-tuple-element.54), calls=%async_computation.2 | async-start | bytes 393216 | tf_op jit(solution)/shard_map/all_to_all | solution.py:408
  141.7 10.4 %all-to-all-done.2.got = f32[16,24,128]{2,1,0:T(8,128)S(1)} async-done(((f32[16,24,128]{2,1,0:T(8,128)}), f32[16,24,128]{2,1,0:T(8,128)S(1)}, u32[]{:S(2)}, u32[]{:S(2)}) %all-to-all-start.2) | async-done | bytes 196640 | tf_op jit(solution)/shard_map/all_to_all | solution.py:408
  152.1 7.2 %update.1 = (bf16[1152,2304]{1,0:T(8,128)(2,1)}, f32[18,128]{1,0:T(8,128)}) custom-call(f32[16,24,128]{2,1,0:T(8,128)S(1)} %all-to-all-done.2.got, f32[9,128]{1,0:T(8,128)S(1)} %get-tuple-element.55.row_new, f32[18,128]{1,0:T(8,128)S(1)} %bitcast.10, f32[1152,2304]{1,0:T(8,128)} %get-tuple-element.56.grad), custom_call_target="tpu_custom_call" | custom-call | tf_op jit(solution)/shard_map/update/pallas_call | solution.py:428
  (104 shorter events, 28.0 us)
Async XLA Ops:
  2.2 25.4 %collective-permute-start = (bf16[128,2304]{1,0:T(8,128)(2,1)S(1)}, bf16[128,2304]{1,0:T(8,128)(2,1)S(1)}, u32[]{:S(2)}, u32[]{:S(2)}) collective-permute-start(bf16[128,2304]{1,0:T(8,128)(2,1)S(1)} %fusion.5.refs_16_), channel_id=1, source_target_pairs={{0,32},{32,64},{64,96},{96,128},{128,160},{160,192},{192,224},{224... | collective-permute-start | bytes 1769480 | tf_op jit(solution)/shard_map/ppermute | solution.py:52
  2.4 25.2 %collective-permute-start.1 = (bf16[128,2304]{1,0:T(8,128)(2,1)S(1)}, bf16[128,2304]{1,0:T(8,128)(2,1)S(1)}, u32[]{:S(2)}, u32[]{:S(2)}) collective-permute-start(bf16[128,2304]{1,0:T(8,128)(2,1)S(1)} %fusion.5.refs_16_), channel_id=1, source_target_pairs={{0,224},{32,0},{64,32},{96,64},{128,96},{160,128},{192,160},{224,1... | collective-permute-start | bytes 1769480 | tf_op jit(solution)/shard_map/ppermute | solution.py:52
  6.5 21.2 %collective-permute-start.2 = (bf16[128,2304]{1,0:T(8,128)(2,1)S(1)}, bf16[128,2304]{1,0:T(8,128)(2,1)S(1)}, u32[]{:S(2)}, u32[]{:S(2)}) collective-permute-start(bf16[128,2304]{1,0:T(8,128)(2,1)S(1)} %fusion.5.refs_16_), channel_id=1, source_target_pairs={{0,16},{16,0},{1,17},{17,1},{2,18},{18,2},{3,19},{19,3},{4,20},{20... | collective-permute-start | bytes 1769480 | tf_op jit(solution)/shard_map/ppermute | solution.py:52
  8.9 18.7 %all-to-all-start = ((bf16[16,72,128]{2,1,0:T(8,128)(2,1)}), bf16[16,72,128]{2,1,0:T(8,128)(2,1)S(1)}, u32[]{:S(2)}, u32[]{:S(2)}) async-start(bf16[16,72,128]{2,1,0:T(8,128)(2,1)} %bitcast.6), calls=%async_computation | async-start | bytes 589824 | tf_op jit(solution)/shard_map/all_to_all | solution.py:83
  28.8 24.4 %collective-permute-start.4 = (bf16[128,3584]{1,0:T(8,128)(2,1)S(1)}, bf16[128,3584]{1,0:T(8,128)(2,1)}, u32[]{:S(2)}, u32[]{:S(2)}) collective-permute-start(bf16[128,3584]{1,0:T(8,128)(2,1)S(1)} %get-tuple-element.64), channel_id=1, source_target_pairs={{0,32},{32,64},{64,96},{96,128},{128,160},{160,192},{192,224},{224... | collective-permute-start | bytes 2752520 | tf_op jit(solution)/shard_map/ppermute | solution.py:52
  32.4 21.8 %collective-permute-start.5 = (bf16[128,3584]{1,0:T(8,128)(2,1)S(1)}, bf16[128,3584]{1,0:T(8,128)(2,1)}, u32[]{:S(2)}, u32[]{:S(2)}) collective-permute-start(bf16[128,3584]{1,0:T(8,128)(2,1)S(1)} %get-tuple-element.63), channel_id=1, source_target_pairs={{0,224},{32,0},{64,32},{96,64},{128,96},{160,128},{192,160},{224,1... | collective-permute-start | bytes 2752520 | tf_op jit(solution)/shard_map/ppermute | solution.py:52
  32.5 11.5 %collective-permute-start.7 = (bf16[8,144,128]{2,1,0:T(8,128)(2,1)S(1)}, bf16[8,144,128]{2,1,0:T(8,128)(2,1)S(1)}, u32[]{:S(2)}, u32[]{:S(2)}) collective-permute-start(bf16[8,144,128]{2,1,0:T(8,128)(2,1)S(1)} %pad_maximum_fusion.6.refs_0_), channel_id=1, source_target_pairs={{0,2},{2,0},{1,3},{3,1},{4,6},{6,4},{5,7},{7,5},{8,10},{10,8},{9,1... | collective-permute-start | bytes 884744 | tf_op jit(solution)/shard_map/ppermute | solution.py:52
  35.5 17.7 %collective-permute-start.6 = (bf16[256,1024]{1,0:T(8,128)(2,1)S(1)}, bf16[256,1024]{1,0:T(8,128)(2,1)S(1)}, u32[]{:S(2)}, u32[]{:S(2)}) collective-permute-start(bf16[256,1024]{1,0:T(8,128)(2,1)S(1)} %pad_maximum_fusion.3), channel_id=1, source_target_pairs={{0,16},{16,0},{1,17},{17,1},{2,18},{18,2},{3,19},{19,3},{4,20},{20... | collective-permute-start | bytes 1572872 | tf_op jit(solution)/shard_map/ppermute | solution.py:52
  35.7 11.0 %collective-permute-start.8 = (bf16[8,144,128]{2,1,0:T(8,128)(2,1)S(1)}, bf16[8,144,128]{2,1,0:T(8,128)(2,1)S(1)}, u32[]{:S(2)}, u32[]{:S(2)}) collective-permute-start(bf16[8,144,128]{2,1,0:T(8,128)(2,1)S(1)} %pad_maximum_fusion.6.refs_0_), channel_id=1, source_target_pairs={{0,4},{4,8},{8,12},{12,0},{1,5},{5,9},{9,13},{13,1},{2,6},{6,10},{... | collective-permute-start | bytes 884744 | tf_op jit(solution)/shard_map/ppermute | solution.py:52
  44.0 7.0 %collective-permute-start.9 = (bf16[8,144,128]{2,1,0:T(8,128)(2,1)S(1)}, bf16[8,144,128]{2,1,0:T(8,128)(2,1)S(1)}, u32[]{:S(2)}, u32[]{:S(2)}) collective-permute-start(bf16[8,144,128]{2,1,0:T(8,128)(2,1)S(1)} %pad_maximum_fusion.6.refs_0_), channel_id=1, source_target_pairs={{0,12},{4,0},{8,4},{12,8},{1,13},{5,1},{9,5},{13,9},{2,14},{6,2},{... | collective-permute-start | bytes 884744 | tf_op jit(solution)/shard_map/ppermute | solution.py:52
  54.2 24.6 %collective-permute-start.22 = (bf16[128,3584]{1,0:T(8,128)(2,1)}, bf16[128,3584]{1,0:T(8,128)(2,1)S(1)}, u32[]{:S(2)}, u32[]{:S(2)}) collective-permute-start(bf16[128,3584]{1,0:T(8,128)(2,1)} %collective-permute-done.4.refs_21_), channel_id=1, source_target_pairs={{0,32},{32,64},{64,96},{96,128},{128,160},{160,192},{192,224},{224... | collective-permute-start | bytes 2752520 | tf_op jit(solution)/shard_map/ppermute | solution.py:52
  55.0 24.3 %collective-permute-start.23 = (bf16[128,3584]{1,0:T(8,128)(2,1)}, bf16[128,3584]{1,0:T(8,128)(2,1)}, u32[]{:S(2)}, u32[]{:S(2)}) collective-permute-start(bf16[128,3584]{1,0:T(8,128)(2,1)} %collective-permute-done.5.refs_22_), channel_id=1, source_target_pairs={{0,224},{32,0},{64,32},{96,64},{128,96},{160,128},{192,160},{224,1... | collective-permute-start | bytes 2752520 | tf_op jit(solution)/shard_map/ppermute | solution.py:52
  59.4 7.2 %collective-permute-start.12 = (bf16[8,144,128]{2,1,0:T(8,128)(2,1)S(1)}, bf16[8,144,128]{2,1,0:T(8,128)(2,1)S(1)}, u32[]{:S(2)}, u32[]{:S(2)}) collective-permute-start(bf16[8,144,128]{2,1,0:T(8,128)(2,1)S(1)} %collective-permute-done.7.refs_4_), channel_id=1, source_target_pairs={{0,12},{4,0},{8,4},{12,8},{1,13},{5,1},{9,5},{13,9},{2,14},{6,2},{... | collective-permute-start | bytes 884744 | tf_op jit(solution)/shard_map/ppermute | solution.py:52
  62.2 9.8 %collective-permute-start.10 = (bf16[8,144,128]{2,1,0:T(8,128)(2,1)S(1)}, bf16[8,144,128]{2,1,0:T(8,128)(2,1)S(1)}, u32[]{:S(2)}, u32[]{:S(2)}) collective-permute-start(bf16[8,144,128]{2,1,0:T(8,128)(2,1)S(1)} %collective-permute-done.8.refs_1_), channel_id=1, source_target_pairs={{0,4},{4,8},{8,12},{12,0},{1,5},{5,9},{9,13},{13,1},{2,6},{6,10},{... | collective-permute-start | bytes 884744 | tf_op jit(solution)/shard_map/ppermute | solution.py:52
  63.1 13.4 %collective-permute-start.24 = (bf16[256,1024]{1,0:T(8,128)(2,1)}, bf16[256,1024]{1,0:T(8,128)(2,1)}, u32[]{:S(2)}, u32[]{:S(2)}) collective-permute-start(bf16[256,1024]{1,0:T(8,128)(2,1)} %pad_maximum_fusion.4), channel_id=1, source_target_pairs={{0,16},{16,0},{1,17},{17,1},{2,18},{18,2},{3,19},{19,3},{4,20},{20... | collective-permute-start | bytes 1572872 | tf_op jit(solution)/shard_map/ppermute | solution.py:52
  66.7 9.8 %collective-permute-start.11 = (bf16[8,144,128]{2,1,0:T(8,128)(2,1)S(1)}, bf16[8,144,128]{2,1,0:T(8,128)(2,1)S(1)}, u32[]{:S(2)}, u32[]{:S(2)}) collective-permute-start(bf16[8,144,128]{2,1,0:T(8,128)(2,1)S(1)} %collective-permute-done.7.refs_4_), channel_id=1, source_target_pairs={{0,4},{4,8},{8,12},{12,0},{1,5},{5,9},{9,13},{13,1},{2,6},{6,10},{... | collective-permute-start | bytes 884744 | tf_op jit(solution)/shard_map/ppermute | solution.py:52
  72.1 6.7 %collective-permute-start.13 = (bf16[8,144,128]{2,1,0:T(8,128)(2,1)S(1)}, bf16[8,144,128]{2,1,0:T(8,128)(2,1)S(1)}, u32[]{:S(2)}, u32[]{:S(2)}) collective-permute-start(bf16[8,144,128]{2,1,0:T(8,128)(2,1)S(1)} %collective-permute-done.12.refs_6_), channel_id=1, source_target_pairs={{0,12},{4,0},{8,4},{12,8},{1,13},{5,1},{9,5},{13,9},{2,14},{6,2},{... | collective-permute-start | bytes 884744 | tf_op jit(solution)/shard_map/ppermute | solution.py:52
  82.7 21.4 %collective-permute-start.27 = (bf16[256,1024]{1,0:T(8,128)(2,1)S(1)}, bf16[256,1024]{1,0:T(8,128)(2,1)S(1)}, u32[]{:S(2)}, u32[]{:S(2)}) collective-permute-start(bf16[256,1024]{1,0:T(8,128)(2,1)S(1)} %pad_maximum_fusion.5), channel_id=1, source_target_pairs={{0,16},{16,0},{1,17},{17,1},{2,18},{18,2},{3,19},{19,3},{4,20},{20... | collective-permute-start | bytes 1572872 | tf_op jit(solution)/shard_map/ppermute | solution.py:52
  83.5 20.7 %collective-permute-start.25 = (bf16[128,2304]{1,0:T(8,128)(2,1)S(1)}, bf16[128,2304]{1,0:T(8,128)(2,1)S(1)}, u32[]{:S(2)}, u32[]{:S(2)}) collective-permute-start(bf16[128,2304]{1,0:T(8,128)(2,1)S(1)} %pad_maximum_fusion.2), channel_id=1, source_target_pairs={{0,32},{32,64},{64,96},{96,128},{128,160},{160,192},{192,224},{224... | collective-permute-start | bytes 1769480 | tf_op jit(solution)/shard_map/ppermute | solution.py:52
  84.9 19.2 %collective-permute-start.26 = (bf16[128,2560]{1,0:T(8,128)(2,1)S(1)}, bf16[128,2560]{1,0:T(8,128)(2,1)S(1)}, u32[]{:S(2)}, u32[]{:S(2)}) collective-permute-start(bf16[128,2560]{1,0:T(8,128)(2,1)S(1)} %slice.46), channel_id=1, source_target_pairs={{0,224},{32,0},{64,32},{96,64},{128,96},{160,128},{192,160},{224,1... | collective-permute-start | bytes 1966088 | tf_op jit(solution)/shard_map/ppermute | solution.py:52
  104.2 8.7 %collective-permute-start.28 = (bf16[128,1024]{1,0:T(8,128)(2,1)S(1)}, bf16[128,1024]{1,0:T(8,128)(2,1)S(1)}, u32[]{:S(2)}, u32[]{:S(2)}) collective-permute-start(bf16[128,1024]{1,0:T(8,128)(2,1)S(1)} %slice.49), channel_id=1, source_target_pairs={{0,16},{16,0},{1,17},{17,1},{2,18},{18,2},{3,19},{19,3},{4,20},{20... | collective-permute-start | bytes 786440 | tf_op jit(solution)/shard_map/ppermute | solution.py:52
  105.7 7.3 %collective-permute-start.29 = (bf16[128,768]{1,0:T(8,128)(2,1)S(1)}, bf16[128,768]{1,0:T(8,128)(2,1)S(1)}, u32[]{:S(2)}, u32[]{:S(2)}) collective-permute-start(bf16[128,768]{1,0:T(8,128)(2,1)S(1)} %slice.50), channel_id=1, source_target_pairs={{0,32},{32,64},{64,96},{96,128},{128,160},{160,192},{192,224},{224... | collective-permute-start | bytes 589832 | tf_op jit(solution)/shard_map/ppermute | solution.py:52
  123.3 12.9 %all-to-all-start.1 = ((f32[16,9,128]{2,1,0:T(8,128)}), f32[16,9,128]{2,1,0:T(8,128)S(1)}, u32[]{:S(2)}, u32[]{:S(2)}) async-start(f32[16,9,128]{2,1,0:T(8,128)} %get-tuple-element.52), calls=%async_computation.1 | async-start | bytes 262144 | tf_op jit(solution)/shard_map/all_to_all | solution.py:408
  137.0 15.0 %all-to-all-start.2 = ((f32[16,24,128]{2,1,0:T(8,128)}), f32[16,24,128]{2,1,0:T(8,128)S(1)}, u32[]{:S(2)}, u32[]{:S(2)}) async-start(f32[16,24,128]{2,1,0:T(8,128)} %get-tuple-element.54), calls=%async_computation.2 | async-start | bytes 393216 | tf_op jit(solution)/shard_map/all_to_all | solution.py:408
  (27 other events, 173.8 us)

commit v4 on v3

--- a/solution.py
+++ b/solution.py
@@ -26,6 +26,7 @@
 BLOCKS = HID // CB
 A_BLOCKS = 5
 A_COLS = A_BLOCKS * CB
+B_COLS = HID - A_COLS
 SPLIT = 4 * CB
 A_UP = 3 * CB
 EARLY = [(0, 0), (0, 1), (7, 0), (1, 0), (7, 1), (1, 1), (6, 0), (2, 0), (6, 1), (2, 1), (5, 0), (3, 0)]
@@ -36,7 +37,7 @@
     [(EARLY + LATE).index((dz, dy)) for dz in range(8) for dy in range(2)], np.int32
 )
 MIB = 1024 * 1024
-AHEAD = 3
+AHEAD = 5
 LIMIT = 50 * MIB
 
 ANY = pl.BlockSpec(memory_space=pl.ANY)
@@ -66,6 +67,26 @@
 
 def other(v, axis):
     return send(v, axis, 2, 1)
+
+
+def pack_kernel(plan, *refs):
+    for source, row, first, target, at_row, at, width in plan:
+        refs[target][at_row : at_row + TOK, at : at + width] = refs[source][
+            row : row + TOK, first : first + width
+        ]
+
+
+def pack(sources, shapes, plan):
+    n = len(sources)
+    return pl.pallas_call(
+        functools.partial(pack_kernel, [p[:3] + (p[3] + n,) + p[4:] for p in plan]),
+        out_shape=[jax.ShapeDtypeStruct(v, jnp.bfloat16) for v in shapes],
+        in_specs=[VMEM] * n,
+        out_specs=[VMEM] * len(shapes),
+        compiler_params=pltpu.CompilerParams(vmem_limit_bytes=8 * MIB),
+        cost_estimate=pl.CostEstimate(flops=0, bytes_accessed=4 * MIB, transcendentals=0),
+        name="pack",
+    )(*sources)
 
 
 def exchange(hidden, grad_out, pos):
@@ -103,9 +124,18 @@
     mine = [half, f0, b0, o0, far, f1, b1, o1]
     theirs = [other(v, "core") for v in mine]
     u3, d3, y2, f1, o0, o1 = tie(u3, d3, y2, f1, o0, o1)
-    u4 = up_z(jnp.concatenate([cut(u3, 0, SPLIT), cut(u3, HID, HID + A_COLS)], 1))
-    d4 = down_z(cut(d3, SPLIT, HID + A_COLS))
-    y3 = cross(cut(u3, A_COLS, HID), cut(d3, A_COLS, HID))
+    m3, mu, md = pack(
+        [u3, d3],
+        [(2 * TOK, B_COLS), (TOK, SPLIT + A_COLS), (TOK, HID - SPLIT + A_COLS)],
+        [
+            (0, 0, A_COLS, 0, 0, 0, B_COLS),
+            (1, 0, A_COLS, 0, TOK, 0, B_COLS),
+            (0, 0, 0, 1, 0, 0, SPLIT),
+            (0, 0, HID, 1, 0, SPLIT, A_COLS),
+            (1, 0, SPLIT, 2, 0, 0, HID - SPLIT + A_COLS),
+        ],
+    )
+    u4, d4, y3 = up_z(mu), down_z(md), other(m3, "yl")
     features = mine + theirs
     n, m, h, k = BLOCKS, A_BLOCKS, SPLIT // CB, A_UP // CB
     pieces = [

time: 162 us -> 160 us (0.988)
  local copies, waits for them, and re-layouts: 8.23 us -> 4.39 us
  starting transfers between devices: 51.1 us -> 53.7 us
    slice x15 -> x10, local copies, waits for them, and re-layouts: 4.17 us -> 0.11 us  [cut(): return lax.slice_in_dim(v, first, last, axis=1)]
    ppermute x31, starting transfers between devices: 36.4 us -> 38 us  [send(): return lax.ppermute(v, axis, ring(n, s))]
  transfers between devices with their start and end apart: 34 -> 34, of which waited for: 13 -> 12; matrix products, arithmetic and copies ran while one was open for 4% -> 1% of each run, Pallas kernels for 10% -> 10%
where the time goes in v4:
time: 160 us; the launch traced here: 158 us
  waiting for transfers between devices  62.9 us (39%)
  starting transfers between devices  53.7 us (34%)
  Pallas kernels  34.2 us (21%)
  local copies, waits for them, and re-layouts  4.39 us (3%)
  other arithmetic  1.76 us (1%)
    ppermute x31, starting transfers between devices, send(): return lax.ppermute(v, axis, ring(n, s))  38 us
    ppermute x31, waiting for transfers between devices, send(): return lax.ppermute(v, axis, ring(n, s))  31.8 us
    all_to_all x2, waiting for transfers between devices, spread(): return lax.all_to_all(v, axes, 0, 0, tiled=True)  18.3 us
    pallas_call x1, Pallas kernels, early_product(): pl.pallas_call(functools.partial(early_kernel, plan), out_shape=(jax.Shap...  15.9 us
    all_to_all x1, waiting for transfers between devices, exchange(): q = lax.all_to_all(turned, DP, 0, 0, tiled=True)  12.8 us
    pallas_call x1, Pallas kernels, late_product(): pl.pallas_call(functools.partial(late_kernel, plan, len(arrays)), out_sha...  10.2 us
    all_to_all x2, starting transfers between devices, spread(): return lax.all_to_all(v, axes, 0, 0, tiled=True)  9.85 us
    pallas_call x1, Pallas kernels, body(): pl.pallas_call(update_kernel, out_shape=(jax.ShapeDtypeStruct((OWN, HID),...  7.15 us
  transfers between devices with their start and end apart: 34, of which 12 were waited for; matrix products, arithmetic and copies ran while one was open for 1% of the time, Pallas kernels for 10%

profile of v4, /device:TPU:0, one launch (start us, length us, event | category | flops | bytes accessed | tf_op | source)
XLA Modules:
  0.0 158.2 jit_solution(16511261325164622093)
XLA Ops:
  2.4 4.0 %collective-permute-start.1 = (bf16[128,2304]{1,0:T(8,128)(2,1)S(1)}, bf16[128,2304]{1,0:T(8,128)(2,1)S(1)}, u32[]{:S(2)}, u32[]{:S(2)}) collective-permute-start(bf16[128,2304]{1,0:T(8,128)(2,1)S(1)} %fusion.5.refs_16_), channel_id=1, source_target_pairs={{0,224},{32,0},{64,32},{96,64},{128,96},{160,128},{192,160},{224,1... | collective-permute-start | bytes 1769480 | tf_op jit(solution)/shard_map/ppermute | solution.py:53
  8.9 5.9 %all-to-all-start = ((bf16[16,72,128]{2,1,0:T(8,128)(2,1)}), bf16[16,72,128]{2,1,0:T(8,128)(2,1)S(1)}, u32[]{:S(2)}, u32[]{:S(2)}) async-start(bf16[16,72,128]{2,1,0:T(8,128)(2,1)} %bitcast.6), calls=%async_computation | async-start | bytes 589824 | tf_op jit(solution)/shard_map/all_to_all | solution.py:104
  14.8 12.8 %all-to-all-done = bf16[16,72,128]{2,1,0:T(8,128)(2,1)S(1)} async-done(((bf16[16,72,128]{2,1,0:T(8,128)(2,1)}), bf16[16,72,128]{2,1,0:T(8,128)(2,1)S(1)}, u32[]{:S(2)}, u32[]{:S(2)}) %all-to-all-start) | async-done | bytes 294944 | tf_op jit(solution)/shard_map/all_to_all | solution.py:104
  28.8 3.6 %collective-permute-start.4 = (bf16[128,3584]{1,0:T(8,128)(2,1)S(1)}, bf16[128,3584]{1,0:T(8,128)(2,1)S(1)}, u32[]{:S(2)}, u32[]{:S(2)}) collective-permute-start(bf16[128,3584]{1,0:T(8,128)(2,1)S(1)} %get-tuple-element.68), channel_id=1, source_target_pairs={{0,32},{32,64},{64,96},{96,128},{128,160},{160,192},{192,224},{224... | collective-permute-start | bytes 2752520 | tf_op jit(solution)/shard_map/ppermute | solution.py:53
  32.5 3.0 %collective-permute-start.7 = (bf16[8,144,128]{2,1,0:T(8,128)(2,1)S(1)}, bf16[8,144,128]{2,1,0:T(8,128)(2,1)S(1)}, u32[]{:S(2)}, u32[]{:S(2)}) collective-permute-start(bf16[8,144,128]{2,1,0:T(8,128)(2,1)S(1)} %pad_maximum_fusion.4.refs_0_), channel_id=1, source_target_pairs={{0,2},{2,0},{1,3},{3,1},{4,6},{6,4},{5,7},{7,5},{8,10},{10,8},{9,1... | collective-permute-start | bytes 884744 | tf_op jit(solution)/shard_map/ppermute | solution.py:53
  37.2 6.8 %collective-permute-done.7.refs_4_ = bf16[8,144,128]{2,1,0:T(8,128)(2,1)S(1)} collective-permute-done((bf16[8,144,128]{2,1,0:T(8,128)(2,1)S(1)}, bf16[8,144,128]{2,1,0:T(8,128)(2,1)S(1)}, u32[]{:S(2)}, u32[]{:S(2)}) %collective-permute-start.7) | collective-permute-done | bytes 294944 | tf_op jit(solution)/shard_map/ppermute | solution.py:53
  44.0 2.8 %collective-permute-start.9 = (bf16[8,144,128]{2,1,0:T(8,128)(2,1)S(1)}, bf16[8,144,128]{2,1,0:T(8,128)(2,1)S(1)}, u32[]{:S(2)}, u32[]{:S(2)}) collective-permute-start(bf16[8,144,128]{2,1,0:T(8,128)(2,1)S(1)} %pad_maximum_fusion.4.refs_0_), channel_id=1, source_target_pairs={{0,12},{4,0},{8,4},{12,8},{1,13},{5,1},{9,5},{13,9},{2,14},{6,2},{... | collective-permute-start | bytes 884744 | tf_op jit(solution)/shard_map/ppermute | solution.py:53
  46.8 4.2 %collective-permute-done.9.refs_2_ = bf16[8,144,128]{2,1,0:T(8,128)(2,1)S(1)} collective-permute-done((bf16[8,144,128]{2,1,0:T(8,128)(2,1)S(1)}, bf16[8,144,128]{2,1,0:T(8,128)(2,1)S(1)}, u32[]{:S(2)}, u32[]{:S(2)}) %collective-permute-start.9) | collective-permute-done | bytes 294944 | tf_op jit(solution)/shard_map/ppermute | solution.py:53
  51.0 2.2 %collective-permute-done.6.refs_20_ = bf16[256,1024]{1,0:T(8,128)(2,1)S(1)} collective-permute-done((bf16[256,1024]{1,0:T(8,128)(2,1)S(1)}, bf16[256,1024]{1,0:T(8,128)(2,1)S(1)}, u32[]{:S(2)}, u32[]{:S(2)}) %collective-permute-start.6) | collective-permute-done | bytes 524320 | tf_op jit(solution)/shard_map/ppermute | solution.py:53
  56.5 2.3 %collective-permute-start.23 = (bf16[128,3584]{1,0:T(8,128)(2,1)S(1)}, bf16[128,3584]{1,0:T(8,128)(2,1)S(1)}, u32[]{:S(2)}, u32[]{:S(2)}) collective-permute-start(bf16[128,3584]{1,0:T(8,128)(2,1)S(1)} %collective-permute-done.5.refs_22_), channel_id=1, source_target_pairs={{0,224},{32,0},{64,32},{96,64},{128,96},{160,128},{192,160},{224,1... | collective-permute-start | bytes 2752520 | tf_op jit(solution)/shard_map/ppermute | solution.py:53
  60.4 2.0 %collective-permute-start.12 = (bf16[8,144,128]{2,1,0:T(8,128)(2,1)S(1)}, bf16[8,144,128]{2,1,0:T(8,128)(2,1)}, u32[]{:S(2)}, u32[]{:S(2)}) collective-permute-start(bf16[8,144,128]{2,1,0:T(8,128)(2,1)S(1)} %collective-permute-done.7.refs_4_), channel_id=1, source_target_pairs={{0,12},{4,0},{8,4},{12,8},{1,13},{5,1},{9,5},{13,9},{2,14},{6,2},{... | collective-permute-start | bytes 884744 | tf_op jit(solution)/shard_map/ppermute | solution.py:53
  62.4 2.9 %collective-permute-done.10.refs_3_ = bf16[8,144,128]{2,1,0:T(8,128)(2,1)} collective-permute-done((bf16[8,144,128]{2,1,0:T(8,128)(2,1)S(1)}, bf16[8,144,128]{2,1,0:T(8,128)(2,1)}, u32[]{:S(2)}, u32[]{:S(2)}) %collective-permute-start.10) | collective-permute-done | bytes 294944 | tf_op jit(solution)/shard_map/ppermute | solution.py:53
  65.3 3.9 %collective-permute-done.11.refs_5_ = bf16[8,144,128]{2,1,0:T(8,128)(2,1)} collective-permute-done((bf16[8,144,128]{2,1,0:T(8,128)(2,1)S(1)}, bf16[8,144,128]{2,1,0:T(8,128)(2,1)}, u32[]{:S(2)}, u32[]{:S(2)}) %collective-permute-start.11) | collective-permute-done | bytes 294944 | tf_op jit(solution)/shard_map/ppermute | solution.py:53
  73.5 7.3 %collective-permute-done.24.refs_23_ = bf16[256,1024]{1,0:T(8,128)(2,1)S(1)} collective-permute-done((bf16[256,1024]{1,0:T(8,128)(2,1)S(1)}, bf16[256,1024]{1,0:T(8,128)(2,1)S(1)}, u32[]{:S(2)}, u32[]{:S(2)}) %collective-permute-start.24) | collective-permute-done | bytes 524320 | tf_op jit(solution)/shard_map/ppermute | solution.py:53
  83.2 2.3 %collective-permute-start.26 = (bf16[128,2560]{1,0:T(8,128)(2,1)S(1)}, bf16[128,2560]{1,0:T(8,128)(2,1)S(1)}, u32[]{:S(2)}, u32[]{:S(2)}) collective-permute-start(bf16[128,2560]{1,0:T(8,128)(2,1)S(1)} %get-tuple-element.51), channel_id=1, source_target_pairs={{0,224},{32,0},{64,32},{96,64},{128,96},{160,128},{192,160},{224,1... | collective-permute-start | bytes 1966088 | tf_op jit(solution)/shard_map/ppermute | solution.py:53
  86.6 15.9 %early.1 = (f32[1152,2304]{1,0:T(8,128)}, bf16[1152,512]{1,0:T(8,128)(2,1)}) custom-call(s32[5]{0:T(128)S(1)} %stack.23.pos, s32[16]{0:T(128)S(1)} %copy-done.8, bf16[8,144,128]{2,1,0:T(8,128)(2,1)S(1)} %pad_maximum_fusion.4.refs_0_, bf16[8,144,128]{2,1,0:T(8,128)(2,1)S(1)} %collective-permute-done.8.refs_1_, ...), custom_call_target="tpu_custom_call" | custom-call | flops 8153726976 | bytes 22413312 | tf_op jit(solution)/shard_map/early/pallas_call | solution.py:274
  103.8 3.5 %collective-permute-start.30 = (bf16[128,512]{1,0:T(8,128)(2,1)S(1)}, bf16[128,512]{1,0:T(8,128)(2,1)S(1)}, u32[]{:S(2)}, u32[]{:S(2)}) collective-permute-start(bf16[128,512]{1,0:T(8,128)(2,1)S(1)} %slice.31), channel_id=1, source_target_pairs={{0,224},{32,0},{64,32},{96,64},{128,96},{160,128},{192,160},{224,1... | collective-permute-start | bytes 393224 | tf_op jit(solution)/shard_map/ppermute | solution.py:53
  107.3 2.5 %collective-permute-done.30.refs_5_ = bf16[128,512]{1,0:T(8,128)(2,1)S(1)} collective-permute-done((bf16[128,512]{1,0:T(8,128)(2,1)S(1)}, bf16[128,512]{1,0:T(8,128)(2,1)S(1)}, u32[]{:S(2)}, u32[]{:S(2)}) %collective-permute-start.30) | collective-permute-done | bytes 131104 | tf_op jit(solution)/shard_map/ppermute | solution.py:53
  110.9 10.2 %late.1 = (f32[1152,2304]{1,0:T(8,128)}, f32[16,9,128]{2,1,0:T(8,128)}, f32[18,128]{1,0:T(8,128)S(1)}) custom-call(s32[5]{0:T(128)S(1)} %stack.23.pos, bf16[1152,512]{1,0:T(8,128)(2,1)S(1)} %copy-done, f32[1152,2304]{1,0:T(8,128)} %get-tuple-element.54.before, bf16[256,1024]{1,0:T(8,128)(2,1)S(1)} %collective-permute-done.27.refs_0_, ...), custom_call_target="tpu_custom_call" | custom-call | flops 2717908992 | bytes 23592960 | tf_op jit(solution)/shard_map/late/pallas_call | solution.py:361
  121.1 6.0 %all-to-all-start.1 = ((f32[16,9,128]{2,1,0:T(8,128)}), f32[16,9,128]{2,1,0:T(8,128)S(1)}, u32[]{:S(2)}, u32[]{:S(2)}) async-start(f32[16,9,128]{2,1,0:T(8,128)} %get-tuple-element.58), calls=%async_computation.1 | async-start | bytes 262144 | tf_op jit(solution)/shard_map/all_to_all | solution.py:438
  127.2 7.9 %all-to-all-done.1.got = f32[16,9,128]{2,1,0:T(8,128)S(1)} async-done(((f32[16,9,128]{2,1,0:T(8,128)}), f32[16,9,128]{2,1,0:T(8,128)S(1)}, u32[]{:S(2)}, u32[]{:S(2)}) %all-to-all-start.1) | async-done | bytes 73760 | tf_op jit(solution)/shard_map/all_to_all | solution.py:438
  135.8 3.9 %all-to-all-start.2 = ((f32[16,24,128]{2,1,0:T(8,128)}), f32[16,24,128]{2,1,0:T(8,128)S(1)}, u32[]{:S(2)}, u32[]{:S(2)}) async-start(f32[16,24,128]{2,1,0:T(8,128)} %get-tuple-element.60), calls=%async_computation.2 | async-start | bytes 393216 | tf_op jit(solution)/shard_map/all_to_all | solution.py:438
  140.4 10.4 %all-to-all-done.2.got = f32[16,24,128]{2,1,0:T(8,128)S(1)} async-done(((f32[16,24,128]{2,1,0:T(8,128)}), f32[16,24,128]{2,1,0:T(8,128)S(1)}, u32[]{:S(2)}, u32[]{:S(2)}) %all-to-all-start.2) | async-done | bytes 196640 | tf_op jit(solution)/shard_map/all_to_all | solution.py:438
  150.8 7.1 %update.1 = (bf16[1152,2304]{1,0:T(8,128)(2,1)}, f32[18,128]{1,0:T(8,128)}) custom-call(f32[16,24,128]{2,1,0:T(8,128)S(1)} %all-to-all-done.2.got, f32[9,128]{1,0:T(8,128)S(1)} %get-tuple-element.61.row_new, f32[18,128]{1,0:T(8,128)S(1)} %bitcast.10, f32[1152,2304]{1,0:T(8,128)} %get-tuple-element.62.grad), custom_call_target="tpu_custom_call" | custom-call | tf_op jit(solution)/shard_map/update/pallas_call | solution.py:458
  (108 shorter events, 23.6 us)
Async XLA Ops:
  2.2 25.4 %collective-permute-start = (bf16[128,2304]{1,0:T(8,128)(2,1)S(1)}, bf16[128,2304]{1,0:T(8,128)(2,1)S(1)}, u32[]{:S(2)}, u32[]{:S(2)}) collective-permute-start(bf16[128,2304]{1,0:T(8,128)(2,1)S(1)} %fusion.5.refs_16_), channel_id=1, source_target_pairs={{0,32},{32,64},{64,96},{96,128},{128,160},{160,192},{192,224},{224... | collective-permute-start | bytes 1769480 | tf_op jit(solution)/shard_map/ppermute | solution.py:53
  2.4 25.2 %collective-permute-start.1 = (bf16[128,2304]{1,0:T(8,128)(2,1)S(1)}, bf16[128,2304]{1,0:T(8,128)(2,1)S(1)}, u32[]{:S(2)}, u32[]{:S(2)}) collective-permute-start(bf16[128,2304]{1,0:T(8,128)(2,1)S(1)} %fusion.5.refs_16_), channel_id=1, source_target_pairs={{0,224},{32,0},{64,32},{96,64},{128,96},{160,128},{192,160},{224,1... | collective-permute-start | bytes 1769480 | tf_op jit(solution)/shard_map/ppermute | solution.py:53
  6.5 21.2 %collective-permute-start.2 = (bf16[128,2304]{1,0:T(8,128)(2,1)S(1)}, bf16[128,2304]{1,0:T(8,128)(2,1)S(1)}, u32[]{:S(2)}, u32[]{:S(2)}) collective-permute-start(bf16[128,2304]{1,0:T(8,128)(2,1)S(1)} %fusion.5.refs_16_), channel_id=1, source_target_pairs={{0,16},{16,0},{1,17},{17,1},{2,18},{18,2},{3,19},{19,3},{4,20},{20... | collective-permute-start | bytes 1769480 | tf_op jit(solution)/shard_map/ppermute | solution.py:53
  8.9 18.7 %all-to-all-start = ((bf16[16,72,128]{2,1,0:T(8,128)(2,1)}), bf16[16,72,128]{2,1,0:T(8,128)(2,1)S(1)}, u32[]{:S(2)}, u32[]{:S(2)}) async-start(bf16[16,72,128]{2,1,0:T(8,128)(2,1)} %bitcast.6), calls=%async_computation | async-start | bytes 589824 | tf_op jit(solution)/shard_map/all_to_all | solution.py:104
  28.8 24.4 %collective-permute-start.4 = (bf16[128,3584]{1,0:T(8,128)(2,1)S(1)}, bf16[128,3584]{1,0:T(8,128)(2,1)S(1)}, u32[]{:S(2)}, u32[]{:S(2)}) collective-permute-start(bf16[128,3584]{1,0:T(8,128)(2,1)S(1)} %get-tuple-element.68), channel_id=1, source_target_pairs={{0,32},{32,64},{64,96},{96,128},{128,160},{160,192},{192,224},{224... | collective-permute-start | bytes 2752520 | tf_op jit(solution)/shard_map/ppermute | solution.py:53
  32.4 21.7 %collective-permute-start.5 = (bf16[128,3584]{1,0:T(8,128)(2,1)S(1)}, bf16[128,3584]{1,0:T(8,128)(2,1)S(1)}, u32[]{:S(2)}, u32[]{:S(2)}) collective-permute-start(bf16[128,3584]{1,0:T(8,128)(2,1)S(1)} %get-tuple-element.67), channel_id=1, source_target_pairs={{0,224},{32,0},{64,32},{96,64},{128,96},{160,128},{192,160},{224,1... | collective-permute-start | bytes 2752520 | tf_op jit(solution)/shard_map/ppermute | solution.py:53
  32.5 11.5 %collective-permute-start.7 = (bf16[8,144,128]{2,1,0:T(8,128)(2,1)S(1)}, bf16[8,144,128]{2,1,0:T(8,128)(2,1)S(1)}, u32[]{:S(2)}, u32[]{:S(2)}) collective-permute-start(bf16[8,144,128]{2,1,0:T(8,128)(2,1)S(1)} %pad_maximum_fusion.4.refs_0_), channel_id=1, source_target_pairs={{0,2},{2,0},{1,3},{3,1},{4,6},{6,4},{5,7},{7,5},{8,10},{10,8},{9,1... | collective-permute-start | bytes 884744 | tf_op jit(solution)/shard_map/ppermute | solution.py:53
  35.5 17.7 %collective-permute-start.6 = (bf16[256,1024]{1,0:T(8,128)(2,1)S(1)}, bf16[256,1024]{1,0:T(8,128)(2,1)S(1)}, u32[]{:S(2)}, u32[]{:S(2)}) collective-permute-start(bf16[256,1024]{1,0:T(8,128)(2,1)S(1)} %pad_maximum_fusion.2), channel_id=1, source_target_pairs={{0,16},{16,0},{1,17},{17,1},{2,18},{18,2},{3,19},{19,3},{4,20},{20... | collective-permute-start | bytes 1572872 | tf_op jit(solution)/shard_map/ppermute | solution.py:53
  35.7 11.0 %collective-permute-start.8 = (bf16[8,144,128]{2,1,0:T(8,128)(2,1)S(1)}, bf16[8,144,128]{2,1,0:T(8,128)(2,1)S(1)}, u32[]{:S(2)}, u32[]{:S(2)}) collective-permute-start(bf16[8,144,128]{2,1,0:T(8,128)(2,1)S(1)} %pad_maximum_fusion.4.refs_0_), channel_id=1, source_target_pairs={{0,4},{4,8},{8,12},{12,0},{1,5},{5,9},{9,13},{13,1},{2,6},{6,10},{... | collective-permute-start | bytes 884744 | tf_op jit(solution)/shard_map/ppermute | solution.py:53
  46.8 13.6 %collective-permute-start.14 = (bf16[8,144,128]{2,1,0:T(8,128)(2,1)S(1)}, bf16[8,144,128]{2,1,0:T(8,128)(2,1)S(1)}, u32[]{:S(2)}, u32[]{:S(2)}) collective-permute-start(bf16[8,144,128]{2,1,0:T(8,128)(2,1)S(1)} %pad_maximum_fusion.4.refs_0_), channel_id=1, source_target_pairs={{0,1},{1,0},{2,3},{3,2},{4,5},{5,4},{6,7},{7,6},{8,9},{9,8},{10,11... | collective-permute-start | bytes 884744 | tf_op jit(solution)/shard_map/ppermute | solution.py:53
  54.1 11.1 %collective-permute-start.10 = (bf16[8,144,128]{2,1,0:T(8,128)(2,1)S(1)}, bf16[8,144,128]{2,1,0:T(8,128)(2,1)}, u32[]{:S(2)}, u32[]{:S(2)}) collective-permute-start(bf16[8,144,128]{2,1,0:T(8,128)(2,1)S(1)} %collective-permute-done.8.refs_1_), channel_id=1, source_target_pairs={{0,4},{4,8},{8,12},{12,0},{1,5},{5,9},{9,13},{13,1},{2,6},{6,10},{... | collective-permute-start | bytes 884744 | tf_op jit(solution)/shard_map/ppermute | solution.py:53
  55.6 25.7 %collective-permute-start.22 = (bf16[128,3584]{1,0:T(8,128)(2,1)S(1)}, bf16[128,3584]{1,0:T(8,128)(2,1)S(1)}, u32[]{:S(2)}, u32[]{:S(2)}) collective-permute-start(bf16[128,3584]{1,0:T(8,128)(2,1)S(1)} %collective-permute-done.4.refs_21_), channel_id=1, source_target_pairs={{0,32},{32,64},{64,96},{96,128},{128,160},{160,192},{192,224},{224... | collective-permute-start | bytes 2752520 | tf_op jit(solution)/shard_map/ppermute | solution.py:53
  56.5 24.9 %collective-permute-start.23 = (bf16[128,3584]{1,0:T(8,128)(2,1)S(1)}, bf16[128,3584]{1,0:T(8,128)(2,1)S(1)}, u32[]{:S(2)}, u32[]{:S(2)}) collective-permute-start(bf16[128,3584]{1,0:T(8,128)(2,1)S(1)} %collective-permute-done.5.refs_22_), channel_id=1, source_target_pairs={{0,224},{32,0},{64,32},{96,64},{128,96},{160,128},{192,160},{224,1... | collective-permute-start | bytes 2752520 | tf_op jit(solution)/shard_map/ppermute | solution.py:53
  58.9 10.4 %collective-permute-start.11 = (bf16[8,144,128]{2,1,0:T(8,128)(2,1)S(1)}, bf16[8,144,128]{2,1,0:T(8,128)(2,1)}, u32[]{:S(2)}, u32[]{:S(2)}) collective-permute-start(bf16[8,144,128]{2,1,0:T(8,128)(2,1)S(1)} %collective-permute-done.7.refs_4_), channel_id=1, source_target_pairs={{0,4},{4,8},{8,12},{12,0},{1,5},{5,9},{9,13},{13,1},{2,6},{6,10},{... | collective-permute-start | bytes 884744 | tf_op jit(solution)/shard_map/ppermute | solution.py:53
  60.4 9.9 %collective-permute-start.12 = (bf16[8,144,128]{2,1,0:T(8,128)(2,1)S(1)}, bf16[8,144,128]{2,1,0:T(8,128)(2,1)}, u32[]{:S(2)}, u32[]{:S(2)}) collective-permute-start(bf16[8,144,128]{2,1,0:T(8,128)(2,1)S(1)} %collective-permute-done.7.refs_4_), channel_id=1, source_target_pairs={{0,12},{4,0},{8,4},{12,8},{1,13},{5,1},{9,5},{13,9},{2,14},{6,2},{... | collective-permute-start | bytes 884744 | tf_op jit(solution)/shard_map/ppermute | solution.py:53
  69.2 11.6 %collective-permute-start.24 = (bf16[256,1024]{1,0:T(8,128)(2,1)S(1)}, bf16[256,1024]{1,0:T(8,128)(2,1)S(1)}, u32[]{:S(2)}, u32[]{:S(2)}) collective-permute-start(bf16[256,1024]{1,0:T(8,128)(2,1)S(1)} %pad_maximum_fusion.3), channel_id=1, source_target_pairs={{0,16},{16,0},{1,17},{17,1},{2,18},{18,2},{3,19},{19,3},{4,20},{20... | collective-permute-start | bytes 1572872 | tf_op jit(solution)/shard_map/ppermute | solution.py:53
  71.0 9.8 %collective-permute-start.13 = (bf16[8,144,128]{2,1,0:T(8,128)(2,1)}, bf16[8,144,128]{2,1,0:T(8,128)(2,1)}, u32[]{:S(2)}, u32[]{:S(2)}) collective-permute-start(bf16[8,144,128]{2,1,0:T(8,128)(2,1)} %collective-permute-done.12.refs_6_), channel_id=1, source_target_pairs={{0,12},{4,0},{8,4},{12,8},{1,13},{5,1},{9,5},{13,9},{2,14},{6,2},{... | collective-permute-start | bytes 884744 | tf_op jit(solution)/shard_map/ppermute | solution.py:53
  73.3 8.9 %collective-permute-start.18 = (bf16[8,144,128]{2,1,0:T(8,128)(2,1)S(1)}, bf16[8,144,128]{2,1,0:T(8,128)(2,1)}, u32[]{:S(2)}, u32[]{:S(2)}) collective-permute-start(bf16[8,144,128]{2,1,0:T(8,128)(2,1)S(1)} %collective-permute-done.7.refs_4_), channel_id=1, source_target_pairs={{0,1},{1,0},{2,3},{3,2},{4,5},{5,4},{6,7},{7,6},{8,9},{9,8},{10,11... | collective-permute-start | bytes 884744 | tf_op jit(solution)/shard_map/ppermute | solution.py:53
  82.2 20.4 %collective-permute-start.25 = (bf16[128,2304]{1,0:T(8,128)(2,1)S(1)}, bf16[128,2304]{1,0:T(8,128)(2,1)S(1)}, u32[]{:S(2)}, u32[]{:S(2)}) collective-permute-start(bf16[128,2304]{1,0:T(8,128)(2,1)S(1)} %get-tuple-element.50), channel_id=1, source_target_pairs={{0,32},{32,64},{64,96},{96,128},{128,160},{160,192},{192,224},{224... | collective-permute-start | bytes 1769480 | tf_op jit(solution)/shard_map/ppermute | solution.py:53
  83.2 19.3 %collective-permute-start.26 = (bf16[128,2560]{1,0:T(8,128)(2,1)S(1)}, bf16[128,2560]{1,0:T(8,128)(2,1)S(1)}, u32[]{:S(2)}, u32[]{:S(2)}) collective-permute-start(bf16[128,2560]{1,0:T(8,128)(2,1)S(1)} %get-tuple-element.51), channel_id=1, source_target_pairs={{0,224},{32,0},{64,32},{96,64},{128,96},{160,128},{192,160},{224,1... | collective-permute-start | bytes 1966088 | tf_op jit(solution)/shard_map/ppermute | solution.py:53
  85.5 17.0 %collective-permute-start.27 = (bf16[256,1024]{1,0:T(8,128)(2,1)S(1)}, bf16[256,1024]{1,0:T(8,128)(2,1)S(1)}, u32[]{:S(2)}, u32[]{:S(2)}) collective-permute-start(bf16[256,1024]{1,0:T(8,128)(2,1)S(1)} %get-tuple-element.52), channel_id=1, source_target_pairs={{0,16},{16,0},{1,17},{17,1},{2,18},{18,2},{3,19},{19,3},{4,20},{20... | collective-permute-start | bytes 1572872 | tf_op jit(solution)/shard_map/ppermute | solution.py:53
  102.6 8.2 %collective-permute-start.28 = (bf16[128,1024]{1,0:T(8,128)(2,1)S(1)}, bf16[128,1024]{1,0:T(8,128)(2,1)S(1)}, u32[]{:S(2)}, u32[]{:S(2)}) collective-permute-start(bf16[128,1024]{1,0:T(8,128)(2,1)S(1)} %slice.29), channel_id=1, source_target_pairs={{0,16},{16,0},{1,17},{17,1},{2,18},{18,2},{3,19},{19,3},{4,20},{20... | collective-permute-start | bytes 786440 | tf_op jit(solution)/shard_map/ppermute | solution.py:53
  121.1 13.9 %all-to-all-start.1 = ((f32[16,9,128]{2,1,0:T(8,128)}), f32[16,9,128]{2,1,0:T(8,128)S(1)}, u32[]{:S(2)}, u32[]{:S(2)}) async-start(f32[16,9,128]{2,1,0:T(8,128)} %get-tuple-element.58), calls=%async_computation.1 | async-start | bytes 262144 | tf_op jit(solution)/shard_map/all_to_all | solution.py:438
  135.8 15.0 %all-to-all-start.2 = ((f32[16,24,128]{2,1,0:T(8,128)}), f32[16,24,128]{2,1,0:T(8,128)S(1)}, u32[]{:S(2)}, u32[]{:S(2)}) async-start(f32[16,24,128]{2,1,0:T(8,128)} %get-tuple-element.60), calls=%async_computation.2 | async-start | bytes 393216 | tf_op jit(solution)/shard_map/all_to_all | solution.py:438
  (31 other events, 290.1 us)

commit v5 on v4

--- a/solution.py
+++ b/solution.py
@@ -212,17 +212,19 @@
     for k in range(16):
         pltpu.make_async_copy(features[k], stages[k], fsem.at[k]).start()
     issue(jnp.int32(0), 0)
+    cols = []
+    for half in (core, 1 - core):
+        for i in range(8):
+            dz = lax.rem(half * 4 + (8 + i // 2) - z, 8)
+            dy = lax.rem((2 + i % 2) - yl, 2)
+            cols.append(pl.multiple_of(places[dz * 2 + dy] * TOK, TOK))
     for k in range(16):
-        pltpu.make_async_copy(features[k], stages[k], fsem.at[k]).wait()
-        half = core if k < 8 else 1 - core
         dx, dy = (0, 3, 1, 2)[k % 4], (k // 4) % 2
         row = (lax.rem(x + dx, 4) * 2 + lax.rem(yh + dy, 2)) * (2 * WID)
         row = pl.multiple_of(row, 16)
+        pltpu.make_async_copy(features[k], stages[k], fsem.at[k]).wait()
         for i in range(8):
-            s = half * 8 + i
-            dz = lax.rem(s // 2 + 8 - z, 8)
-            dy = lax.rem(lax.rem(s, 2) + 2 - yl, 2)
-            col = pl.multiple_of(places[dz * 2 + dy] * TOK, TOK)
+            col = cols[k // 8 * 8 + i]
             lhs[pl.ds(row, 2 * WID), pl.ds(col, TOK)] = stages[k][i]
     late_copy = pltpu.make_async_copy(lhs.at[:, EARLY_TOK:], lhs_late, lsem)
     late_copy.start()

time: 160 us -> 160 us (level)
  no operation moved by 1% of the time
where the time goes in v5:
time: 160 us; the launch traced here: 158 us
  waiting for transfers between devices  62.9 us (39%)
  starting transfers between devices  53.7 us (34%)
  Pallas kernels  34.2 us (21%)
  local copies, waits for them, and re-layouts  4.39 us (3%)
  other arithmetic  1.76 us (1%)
    ppermute x31, starting transfers between devices, send(): return lax.ppermute(v, axis, ring(n, s))  38 us
    ppermute x31, waiting for transfers between devices, send(): return lax.ppermute(v, axis, ring(n, s))  31.8 us
    all_to_all x2, waiting for transfers between devices, spread(): return lax.all_to_all(v, axes, 0, 0, tiled=True)  18.3 us
    pallas_call x1, Pallas kernels, early_product(): pl.pallas_call(functools.partial(early_kernel, plan), out_shape=(jax.Shap...  15.9 us
    all_to_all x1, waiting for transfers between devices, exchange(): q = lax.all_to_all(turned, DP, 0, 0, tiled=True)  12.8 us
    pallas_call x1, Pallas kernels, late_product(): pl.pallas_call(functools.partial(late_kernel, plan, len(arrays)), out_sha...  10.2 us
    all_to_all x2, starting transfers between devices, spread(): return lax.all_to_all(v, axes, 0, 0, tiled=True)  9.85 us
    pallas_call x1, Pallas kernels, body(): pl.pallas_call(update_kernel, out_shape=(jax.ShapeDtypeStruct((OWN, HID),...  7.15 us
  transfers between devices with their start and end apart: 34, of which 12 were waited for; matrix products, arithmetic and copies ran while one was open for 1% of the time, Pallas kernels for 10%

profile of v5, /device:TPU:0, one launch (start us, length us, event | category | flops | bytes accessed | tf_op | source)
XLA Modules:
  0.0 158.1 jit_solution(10337430529909565501)
XLA Ops:
  2.4 4.0 %collective-permute-start.1 = (bf16[128,2304]{1,0:T(8,128)(2,1)S(1)}, bf16[128,2304]{1,0:T(8,128)(2,1)S(1)}, u32[]{:S(2)}, u32[]{:S(2)}) collective-permute-start(bf16[128,2304]{1,0:T(8,128)(2,1)S(1)} %fusion.5.refs_16_), channel_id=1, source_target_pairs={{0,224},{32,0},{64,32},{96,64},{128,96},{160,128},{192,160},{224,1... | collective-permute-start | bytes 1769480 | tf_op jit(solution)/shard_map/ppermute | solution.py:53
  8.9 5.9 %all-to-all-start = ((bf16[16,72,128]{2,1,0:T(8,128)(2,1)}), bf16[16,72,128]{2,1,0:T(8,128)(2,1)S(1)}, u32[]{:S(2)}, u32[]{:S(2)}) async-start(bf16[16,72,128]{2,1,0:T(8,128)(2,1)} %bitcast.6), calls=%async_computation | async-start | bytes 589824 | tf_op jit(solution)/shard_map/all_to_all | solution.py:104
  14.8 12.8 %all-to-all-done = bf16[16,72,128]{2,1,0:T(8,128)(2,1)S(1)} async-done(((bf16[16,72,128]{2,1,0:T(8,128)(2,1)}), bf16[16,72,128]{2,1,0:T(8,128)(2,1)S(1)}, u32[]{:S(2)}, u32[]{:S(2)}) %all-to-all-start) | async-done | bytes 294944 | tf_op jit(solution)/shard_map/all_to_all | solution.py:104
  28.8 3.6 %collective-permute-start.4 = (bf16[128,3584]{1,0:T(8,128)(2,1)S(1)}, bf16[128,3584]{1,0:T(8,128)(2,1)S(1)}, u32[]{:S(2)}, u32[]{:S(2)}) collective-permute-start(bf16[128,3584]{1,0:T(8,128)(2,1)S(1)} %get-tuple-element.68), channel_id=1, source_target_pairs={{0,32},{32,64},{64,96},{96,128},{128,160},{160,192},{192,224},{224... | collective-permute-start | bytes 2752520 | tf_op jit(solution)/shard_map/ppermute | solution.py:53
  32.5 3.0 %collective-permute-start.7 = (bf16[8,144,128]{2,1,0:T(8,128)(2,1)S(1)}, bf16[8,144,128]{2,1,0:T(8,128)(2,1)S(1)}, u32[]{:S(2)}, u32[]{:S(2)}) collective-permute-start(bf16[8,144,128]{2,1,0:T(8,128)(2,1)S(1)} %pad_maximum_fusion.4.refs_0_), channel_id=1, source_target_pairs={{0,2},{2,0},{1,3},{3,1},{4,6},{6,4},{5,7},{7,5},{8,10},{10,8},{9,1... | collective-permute-start | bytes 884744 | tf_op jit(solution)/shard_map/ppermute | solution.py:53
  37.2 6.8 %collective-permute-done.7.refs_4_ = bf16[8,144,128]{2,1,0:T(8,128)(2,1)S(1)} collective-permute-done((bf16[8,144,128]{2,1,0:T(8,128)(2,1)S(1)}, bf16[8,144,128]{2,1,0:T(8,128)(2,1)S(1)}, u32[]{:S(2)}, u32[]{:S(2)}) %collective-permute-start.7) | collective-permute-done | bytes 294944 | tf_op jit(solution)/shard_map/ppermute | solution.py:53
  44.0 2.8 %collective-permute-start.9 = (bf16[8,144,128]{2,1,0:T(8,128)(2,1)S(1)}, bf16[8,144,128]{2,1,0:T(8,128)(2,1)S(1)}, u32[]{:S(2)}, u32[]{:S(2)}) collective-permute-start(bf16[8,144,128]{2,1,0:T(8,128)(2,1)S(1)} %pad_maximum_fusion.4.refs_0_), channel_id=1, source_target_pairs={{0,12},{4,0},{8,4},{12,8},{1,13},{5,1},{9,5},{13,9},{2,14},{6,2},{... | collective-permute-start | bytes 884744 | tf_op jit(solution)/shard_map/ppermute | solution.py:53
  46.8 4.2 %collective-permute-done.9.refs_2_ = bf16[8,144,128]{2,1,0:T(8,128)(2,1)S(1)} collective-permute-done((bf16[8,144,128]{2,1,0:T(8,128)(2,1)S(1)}, bf16[8,144,128]{2,1,0:T(8,128)(2,1)S(1)}, u32[]{:S(2)}, u32[]{:S(2)}) %collective-permute-start.9) | collective-permute-done | bytes 294944 | tf_op jit(solution)/shard_map/ppermute | solution.py:53
  51.0 2.2 %collective-permute-done.6.refs_20_ = bf16[256,1024]{1,0:T(8,128)(2,1)S(1)} collective-permute-done((bf16[256,1024]{1,0:T(8,128)(2,1)S(1)}, bf16[256,1024]{1,0:T(8,128)(2,1)S(1)}, u32[]{:S(2)}, u32[]{:S(2)}) %collective-permute-start.6) | collective-permute-done | bytes 524320 | tf_op jit(solution)/shard_map/ppermute | solution.py:53
  56.5 2.3 %collective-permute-start.23 = (bf16[128,3584]{1,0:T(8,128)(2,1)S(1)}, bf16[128,3584]{1,0:T(8,128)(2,1)S(1)}, u32[]{:S(2)}, u32[]{:S(2)}) collective-permute-start(bf16[128,3584]{1,0:T(8,128)(2,1)S(1)} %collective-permute-done.5.refs_22_), channel_id=1, source_target_pairs={{0,224},{32,0},{64,32},{96,64},{128,96},{160,128},{192,160},{224,1... | collective-permute-start | bytes 2752520 | tf_op jit(solution)/shard_map/ppermute | solution.py:53
  60.4 2.0 %collective-permute-start.12 = (bf16[8,144,128]{2,1,0:T(8,128)(2,1)S(1)}, bf16[8,144,128]{2,1,0:T(8,128)(2,1)}, u32[]{:S(2)}, u32[]{:S(2)}) collective-permute-start(bf16[8,144,128]{2,1,0:T(8,128)(2,1)S(1)} %collective-permute-done.7.refs_4_), channel_id=1, source_target_pairs={{0,12},{4,0},{8,4},{12,8},{1,13},{5,1},{9,5},{13,9},{2,14},{6,2},{... | collective-permute-start | bytes 884744 | tf_op jit(solution)/shard_map/ppermute | solution.py:53
  62.4 2.9 %collective-permute-done.10.refs_3_ = bf16[8,144,128]{2,1,0:T(8,128)(2,1)} collective-permute-done((bf16[8,144,128]{2,1,0:T(8,128)(2,1)S(1)}, bf16[8,144,128]{2,1,0:T(8,128)(2,1)}, u32[]{:S(2)}, u32[]{:S(2)}) %collective-permute-start.10) | collective-permute-done | bytes 294944 | tf_op jit(solution)/shard_map/ppermute | solution.py:53
  65.3 3.9 %collective-permute-done.11.refs_5_ = bf16[8,144,128]{2,1,0:T(8,128)(2,1)} collective-permute-done((bf16[8,144,128]{2,1,0:T(8,128)(2,1)S(1)}, bf16[8,144,128]{2,1,0:T(8,128)(2,1)}, u32[]{:S(2)}, u32[]{:S(2)}) %collective-permute-start.11) | collective-permute-done | bytes 294944 | tf_op jit(solution)/shard_map/ppermute | solution.py:53
  73.5 7.3 %collective-permute-done.24.refs_23_ = bf16[256,1024]{1,0:T(8,128)(2,1)S(1)} collective-permute-done((bf16[256,1024]{1,0:T(8,128)(2,1)S(1)}, bf16[256,1024]{1,0:T(8,128)(2,1)S(1)}, u32[]{:S(2)}, u32[]{:S(2)}) %collective-permute-start.24) | collective-permute-done | bytes 524320 | tf_op jit(solution)/shard_map/ppermute | solution.py:53
  83.2 2.3 %collective-permute-start.26 = (bf16[128,2560]{1,0:T(8,128)(2,1)S(1)}, bf16[128,2560]{1,0:T(8,128)(2,1)S(1)}, u32[]{:S(2)}, u32[]{:S(2)}) collective-permute-start(bf16[128,2560]{1,0:T(8,128)(2,1)S(1)} %get-tuple-element.51), channel_id=1, source_target_pairs={{0,224},{32,0},{64,32},{96,64},{128,96},{160,128},{192,160},{224,1... | collective-permute-start | bytes 1966088 | tf_op jit(solution)/shard_map/ppermute | solution.py:53
  86.6 15.9 %early.1 = (f32[1152,2304]{1,0:T(8,128)}, bf16[1152,512]{1,0:T(8,128)(2,1)}) custom-call(s32[5]{0:T(128)S(1)} %stack.23.pos, s32[16]{0:T(128)S(1)} %copy-done.8, bf16[8,144,128]{2,1,0:T(8,128)(2,1)S(1)} %pad_maximum_fusion.4.refs_0_, bf16[8,144,128]{2,1,0:T(8,128)(2,1)S(1)} %collective-permute-done.8.refs_1_, ...), custom_call_target="tpu_custom_call" | custom-call | flops 8153726976 | bytes 22413312 | tf_op jit(solution)/shard_map/early/pallas_call | solution.py:276
  103.8 3.5 %collective-permute-start.30 = (bf16[128,512]{1,0:T(8,128)(2,1)S(1)}, bf16[128,512]{1,0:T(8,128)(2,1)S(1)}, u32[]{:S(2)}, u32[]{:S(2)}) collective-permute-start(bf16[128,512]{1,0:T(8,128)(2,1)S(1)} %slice.31), channel_id=1, source_target_pairs={{0,224},{32,0},{64,32},{96,64},{128,96},{160,128},{192,160},{224,1... | collective-permute-start | bytes 393224 | tf_op jit(solution)/shard_map/ppermute | solution.py:53
  107.3 2.5 %collective-permute-done.30.refs_5_ = bf16[128,512]{1,0:T(8,128)(2,1)S(1)} collective-permute-done((bf16[128,512]{1,0:T(8,128)(2,1)S(1)}, bf16[128,512]{1,0:T(8,128)(2,1)S(1)}, u32[]{:S(2)}, u32[]{:S(2)}) %collective-permute-start.30) | collective-permute-done | bytes 131104 | tf_op jit(solution)/shard_map/ppermute | solution.py:53
  110.8 10.2 %late.1 = (f32[1152,2304]{1,0:T(8,128)}, f32[16,9,128]{2,1,0:T(8,128)}, f32[18,128]{1,0:T(8,128)S(1)}) custom-call(s32[5]{0:T(128)S(1)} %stack.23.pos, bf16[1152,512]{1,0:T(8,128)(2,1)S(1)} %copy-done, f32[1152,2304]{1,0:T(8,128)} %get-tuple-element.54.before, bf16[256,1024]{1,0:T(8,128)(2,1)S(1)} %collective-permute-done.27.refs_0_, ...), custom_call_target="tpu_custom_call" | custom-call | flops 2717908992 | bytes 23592960 | tf_op jit(solution)/shard_map/late/pallas_call | solution.py:363
  121.1 5.9 %all-to-all-start.1 = ((f32[16,9,128]{2,1,0:T(8,128)}), f32[16,9,128]{2,1,0:T(8,128)S(1)}, u32[]{:S(2)}, u32[]{:S(2)}) async-start(f32[16,9,128]{2,1,0:T(8,128)} %get-tuple-element.58), calls=%async_computation.1 | async-start | bytes 262144 | tf_op jit(solution)/shard_map/all_to_all | solution.py:440
  127.1 7.9 %all-to-all-done.1.got = f32[16,9,128]{2,1,0:T(8,128)S(1)} async-done(((f32[16,9,128]{2,1,0:T(8,128)}), f32[16,9,128]{2,1,0:T(8,128)S(1)}, u32[]{:S(2)}, u32[]{:S(2)}) %all-to-all-start.1) | async-done | bytes 73760 | tf_op jit(solution)/shard_map/all_to_all | solution.py:440
  135.8 3.9 %all-to-all-start.2 = ((f32[16,24,128]{2,1,0:T(8,128)}), f32[16,24,128]{2,1,0:T(8,128)S(1)}, u32[]{:S(2)}, u32[]{:S(2)}) async-start(f32[16,24,128]{2,1,0:T(8,128)} %get-tuple-element.60), calls=%async_computation.2 | async-start | bytes 393216 | tf_op jit(solution)/shard_map/all_to_all | solution.py:440
  140.4 10.4 %all-to-all-done.2.got = f32[16,24,128]{2,1,0:T(8,128)S(1)} async-done(((f32[16,24,128]{2,1,0:T(8,128)}), f32[16,24,128]{2,1,0:T(8,128)S(1)}, u32[]{:S(2)}, u32[]{:S(2)}) %all-to-all-start.2) | async-done | bytes 196640 | tf_op jit(solution)/shard_map/all_to_all | solution.py:440
  150.8 7.1 %update.1 = (bf16[1152,2304]{1,0:T(8,128)(2,1)}, f32[18,128]{1,0:T(8,128)}) custom-call(f32[16,24,128]{2,1,0:T(8,128)S(1)} %all-to-all-done.2.got, f32[9,128]{1,0:T(8,128)S(1)} %get-tuple-element.61.row_new, f32[18,128]{1,0:T(8,128)S(1)} %bitcast.10, f32[1152,2304]{1,0:T(8,128)} %get-tuple-element.62.grad), custom_call_target="tpu_custom_call" | custom-call | tf_op jit(solution)/shard_map/update/pallas_call | solution.py:460
  (108 shorter events, 23.6 us)
Async XLA Ops:
  2.2 25.4 %collective-permute-start = (bf16[128,2304]{1,0:T(8,128)(2,1)S(1)}, bf16[128,2304]{1,0:T(8,128)(2,1)S(1)}, u32[]{:S(2)}, u32[]{:S(2)}) collective-permute-start(bf16[128,2304]{1,0:T(8,128)(2,1)S(1)} %fusion.5.refs_16_), channel_id=1, source_target_pairs={{0,32},{32,64},{64,96},{96,128},{128,160},{160,192},{192,224},{224... | collective-permute-start | bytes 1769480 | tf_op jit(solution)/shard_map/ppermute | solution.py:53
  2.4 25.2 %collective-permute-start.1 = (bf16[128,2304]{1,0:T(8,128)(2,1)S(1)}, bf16[128,2304]{1,0:T(8,128)(2,1)S(1)}, u32[]{:S(2)}, u32[]{:S(2)}) collective-permute-start(bf16[128,2304]{1,0:T(8,128)(2,1)S(1)} %fusion.5.refs_16_), channel_id=1, source_target_pairs={{0,224},{32,0},{64,32},{96,64},{128,96},{160,128},{192,160},{224,1... | collective-permute-start | bytes 1769480 | tf_op jit(solution)/shard_map/ppermute | solution.py:53
  6.5 21.2 %collective-permute-start.2 = (bf16[128,2304]{1,0:T(8,128)(2,1)S(1)}, bf16[128,2304]{1,0:T(8,128)(2,1)S(1)}, u32[]{:S(2)}, u32[]{:S(2)}) collective-permute-start(bf16[128,2304]{1,0:T(8,128)(2,1)S(1)} %fusion.5.refs_16_), channel_id=1, source_target_pairs={{0,16},{16,0},{1,17},{17,1},{2,18},{18,2},{3,19},{19,3},{4,20},{20... | collective-permute-start | bytes 1769480 | tf_op jit(solution)/shard_map/ppermute | solution.py:53
  8.9 18.7 %all-to-all-start = ((bf16[16,72,128]{2,1,0:T(8,128)(2,1)}), bf16[16,72,128]{2,1,0:T(8,128)(2,1)S(1)}, u32[]{:S(2)}, u32[]{:S(2)}) async-start(bf16[16,72,128]{2,1,0:T(8,128)(2,1)} %bitcast.6), calls=%async_computation | async-start | bytes 589824 | tf_op jit(solution)/shard_map/all_to_all | solution.py:104
  28.8 24.4 %collective-permute-start.4 = (bf16[128,3584]{1,0:T(8,128)(2,1)S(1)}, bf16[128,3584]{1,0:T(8,128)(2,1)S(1)}, u32[]{:S(2)}, u32[]{:S(2)}) collective-permute-start(bf16[128,3584]{1,0:T(8,128)(2,1)S(1)} %get-tuple-element.68), channel_id=1, source_target_pairs={{0,32},{32,64},{64,96},{96,128},{128,160},{160,192},{192,224},{224... | collective-permute-start | bytes 2752520 | tf_op jit(solution)/shard_map/ppermute | solution.py:53
  32.4 21.7 %collective-permute-start.5 = (bf16[128,3584]{1,0:T(8,128)(2,1)S(1)}, bf16[128,3584]{1,0:T(8,128)(2,1)S(1)}, u32[]{:S(2)}, u32[]{:S(2)}) collective-permute-start(bf16[128,3584]{1,0:T(8,128)(2,1)S(1)} %get-tuple-element.67), channel_id=1, source_target_pairs={{0,224},{32,0},{64,32},{96,64},{128,96},{160,128},{192,160},{224,1... | collective-permute-start | bytes 2752520 | tf_op jit(solution)/shard_map/ppermute | solution.py:53
  32.5 11.5 %collective-permute-start.7 = (bf16[8,144,128]{2,1,0:T(8,128)(2,1)S(1)}, bf16[8,144,128]{2,1,0:T(8,128)(2,1)S(1)}, u32[]{:S(2)}, u32[]{:S(2)}) collective-permute-start(bf16[8,144,128]{2,1,0:T(8,128)(2,1)S(1)} %pad_maximum_fusion.4.refs_0_), channel_id=1, source_target_pairs={{0,2},{2,0},{1,3},{3,1},{4,6},{6,4},{5,7},{7,5},{8,10},{10,8},{9,1... | collective-permute-start | bytes 884744 | tf_op jit(solution)/shard_map/ppermute | solution.py:53
  35.5 17.7 %collective-permute-start.6 = (bf16[256,1024]{1,0:T(8,128)(2,1)S(1)}, bf16[256,1024]{1,0:T(8,128)(2,1)S(1)}, u32[]{:S(2)}, u32[]{:S(2)}) collective-permute-start(bf16[256,1024]{1,0:T(8,128)(2,1)S(1)} %pad_maximum_fusion.2), channel_id=1, source_target_pairs={{0,16},{16,0},{1,17},{17,1},{2,18},{18,2},{3,19},{19,3},{4,20},{20... | collective-permute-start | bytes 1572872 | tf_op jit(solution)/shard_map/ppermute | solution.py:53
  35.7 11.0 %collective-permute-start.8 = (bf16[8,144,128]{2,1,0:T(8,128)(2,1)S(1)}, bf16[8,144,128]{2,1,0:T(8,128)(2,1)S(1)}, u32[]{:S(2)}, u32[]{:S(2)}) collective-permute-start(bf16[8,144,128]{2,1,0:T(8,128)(2,1)S(1)} %pad_maximum_fusion.4.refs_0_), channel_id=1, source_target_pairs={{0,4},{4,8},{8,12},{12,0},{1,5},{5,9},{9,13},{13,1},{2,6},{6,10},{... | collective-permute-start | bytes 884744 | tf_op jit(solution)/shard_map/ppermute | solution.py:53
  46.8 13.6 %collective-permute-start.14 = (bf16[8,144,128]{2,1,0:T(8,128)(2,1)S(1)}, bf16[8,144,128]{2,1,0:T(8,128)(2,1)S(1)}, u32[]{:S(2)}, u32[]{:S(2)}) collective-permute-start(bf16[8,144,128]{2,1,0:T(8,128)(2,1)S(1)} %pad_maximum_fusion.4.refs_0_), channel_id=1, source_target_pairs={{0,1},{1,0},{2,3},{3,2},{4,5},{5,4},{6,7},{7,6},{8,9},{9,8},{10,11... | collective-permute-start | bytes 884744 | tf_op jit(solution)/shard_map/ppermute | solution.py:53
  54.1 11.1 %collective-permute-start.10 = (bf16[8,144,128]{2,1,0:T(8,128)(2,1)S(1)}, bf16[8,144,128]{2,1,0:T(8,128)(2,1)}, u32[]{:S(2)}, u32[]{:S(2)}) collective-permute-start(bf16[8,144,128]{2,1,0:T(8,128)(2,1)S(1)} %collective-permute-done.8.refs_1_), channel_id=1, source_target_pairs={{0,4},{4,8},{8,12},{12,0},{1,5},{5,9},{9,13},{13,1},{2,6},{6,10},{... | collective-permute-start | bytes 884744 | tf_op jit(solution)/shard_map/ppermute | solution.py:53
  55.6 25.7 %collective-permute-start.22 = (bf16[128,3584]{1,0:T(8,128)(2,1)S(1)}, bf16[128,3584]{1,0:T(8,128)(2,1)S(1)}, u32[]{:S(2)}, u32[]{:S(2)}) collective-permute-start(bf16[128,3584]{1,0:T(8,128)(2,1)S(1)} %collective-permute-done.4.refs_21_), channel_id=1, source_target_pairs={{0,32},{32,64},{64,96},{96,128},{128,160},{160,192},{192,224},{224... | collective-permute-start | bytes 2752520 | tf_op jit(solution)/shard_map/ppermute | solution.py:53
  56.5 24.9 %collective-permute-start.23 = (bf16[128,3584]{1,0:T(8,128)(2,1)S(1)}, bf16[128,3584]{1,0:T(8,128)(2,1)S(1)}, u32[]{:S(2)}, u32[]{:S(2)}) collective-permute-start(bf16[128,3584]{1,0:T(8,128)(2,1)S(1)} %collective-permute-done.5.refs_22_), channel_id=1, source_target_pairs={{0,224},{32,0},{64,32},{96,64},{128,96},{160,128},{192,160},{224,1... | collective-permute-start | bytes 2752520 | tf_op jit(solution)/shard_map/ppermute | solution.py:53
  58.9 10.4 %collective-permute-start.11 = (bf16[8,144,128]{2,1,0:T(8,128)(2,1)S(1)}, bf16[8,144,128]{2,1,0:T(8,128)(2,1)}, u32[]{:S(2)}, u32[]{:S(2)}) collective-permute-start(bf16[8,144,128]{2,1,0:T(8,128)(2,1)S(1)} %collective-permute-done.7.refs_4_), channel_id=1, source_target_pairs={{0,4},{4,8},{8,12},{12,0},{1,5},{5,9},{9,13},{13,1},{2,6},{6,10},{... | collective-permute-start | bytes 884744 | tf_op jit(solution)/shard_map/ppermute | solution.py:53
  60.4 9.9 %collective-permute-start.12 = (bf16[8,144,128]{2,1,0:T(8,128)(2,1)S(1)}, bf16[8,144,128]{2,1,0:T(8,128)(2,1)}, u32[]{:S(2)}, u32[]{:S(2)}) collective-permute-start(bf16[8,144,128]{2,1,0:T(8,128)(2,1)S(1)} %collective-permute-done.7.refs_4_), channel_id=1, source_target_pairs={{0,12},{4,0},{8,4},{12,8},{1,13},{5,1},{9,5},{13,9},{2,14},{6,2},{... | collective-permute-start | bytes 884744 | tf_op jit(solution)/shard_map/ppermute | solution.py:53
  69.2 11.6 %collective-permute-start.24 = (bf16[256,1024]{1,0:T(8,128)(2,1)S(1)}, bf16[256,1024]{1,0:T(8,128)(2,1)S(1)}, u32[]{:S(2)}, u32[]{:S(2)}) collective-permute-start(bf16[256,1024]{1,0:T(8,128)(2,1)S(1)} %pad_maximum_fusion.3), channel_id=1, source_target_pairs={{0,16},{16,0},{1,17},{17,1},{2,18},{18,2},{3,19},{19,3},{4,20},{20... | collective-permute-start | bytes 1572872 | tf_op jit(solution)/shard_map/ppermute | solution.py:53
  71.0 9.8 %collective-permute-start.13 = (bf16[8,144,128]{2,1,0:T(8,128)(2,1)}, bf16[8,144,128]{2,1,0:T(8,128)(2,1)}, u32[]{:S(2)}, u32[]{:S(2)}) collective-permute-start(bf16[8,144,128]{2,1,0:T(8,128)(2,1)} %collective-permute-done.12.refs_6_), channel_id=1, source_target_pairs={{0,12},{4,0},{8,4},{12,8},{1,13},{5,1},{9,5},{13,9},{2,14},{6,2},{... | collective-permute-start | bytes 884744 | tf_op jit(solution)/shard_map/ppermute | solution.py:53
  73.3 8.9 %collective-permute-start.18 = (bf16[8,144,128]{2,1,0:T(8,128)(2,1)S(1)}, bf16[8,144,128]{2,1,0:T(8,128)(2,1)}, u32[]{:S(2)}, u32[]{:S(2)}) collective-permute-start(bf16[8,144,128]{2,1,0:T(8,128)(2,1)S(1)} %collective-permute-done.7.refs_4_), channel_id=1, source_target_pairs={{0,1},{1,0},{2,3},{3,2},{4,5},{5,4},{6,7},{7,6},{8,9},{9,8},{10,11... | collective-permute-start | bytes 884744 | tf_op jit(solution)/shard_map/ppermute | solution.py:53
  82.2 20.3 %collective-permute-start.25 = (bf16[128,2304]{1,0:T(8,128)(2,1)S(1)}, bf16[128,2304]{1,0:T(8,128)(2,1)S(1)}, u32[]{:S(2)}, u32[]{:S(2)}) collective-permute-start(bf16[128,2304]{1,0:T(8,128)(2,1)S(1)} %get-tuple-element.50), channel_id=1, source_target_pairs={{0,32},{32,64},{64,96},{96,128},{128,160},{160,192},{192,224},{224... | collective-permute-start | bytes 1769480 | tf_op jit(solution)/shard_map/ppermute | solution.py:53
  83.2 19.3 %collective-permute-start.26 = (bf16[128,2560]{1,0:T(8,128)(2,1)S(1)}, bf16[128,2560]{1,0:T(8,128)(2,1)S(1)}, u32[]{:S(2)}, u32[]{:S(2)}) collective-permute-start(bf16[128,2560]{1,0:T(8,128)(2,1)S(1)} %get-tuple-element.51), channel_id=1, source_target_pairs={{0,224},{32,0},{64,32},{96,64},{128,96},{160,128},{192,160},{224,1... | collective-permute-start | bytes 1966088 | tf_op jit(solution)/shard_map/ppermute | solution.py:53
  85.5 17.0 %collective-permute-start.27 = (bf16[256,1024]{1,0:T(8,128)(2,1)S(1)}, bf16[256,1024]{1,0:T(8,128)(2,1)S(1)}, u32[]{:S(2)}, u32[]{:S(2)}) collective-permute-start(bf16[256,1024]{1,0:T(8,128)(2,1)S(1)} %get-tuple-element.52), channel_id=1, source_target_pairs={{0,16},{16,0},{1,17},{17,1},{2,18},{18,2},{3,19},{19,3},{4,20},{20... | collective-permute-start | bytes 1572872 | tf_op jit(solution)/shard_map/ppermute | solution.py:53
  102.6 8.2 %collective-permute-start.28 = (bf16[128,1024]{1,0:T(8,128)(2,1)S(1)}, bf16[128,1024]{1,0:T(8,128)(2,1)S(1)}, u32[]{:S(2)}, u32[]{:S(2)}) collective-permute-start(bf16[128,1024]{1,0:T(8,128)(2,1)S(1)} %slice.29), channel_id=1, source_target_pairs={{0,16},{16,0},{1,17},{17,1},{2,18},{18,2},{3,19},{19,3},{4,20},{20... | collective-permute-start | bytes 786440 | tf_op jit(solution)/shard_map/ppermute | solution.py:53
  121.1 13.9 %all-to-all-start.1 = ((f32[16,9,128]{2,1,0:T(8,128)}), f32[16,9,128]{2,1,0:T(8,128)S(1)}, u32[]{:S(2)}, u32[]{:S(2)}) async-start(f32[16,9,128]{2,1,0:T(8,128)} %get-tuple-element.58), calls=%async_computation.1 | async-start | bytes 262144 | tf_op jit(solution)/shard_map/all_to_all | solution.py:440
  135.8 15.0 %all-to-all-start.2 = ((f32[16,24,128]{2,1,0:T(8,128)}), f32[16,24,128]{2,1,0:T(8,128)S(1)}, u32[]{:S(2)}, u32[]{:S(2)}) async-start(f32[16,24,128]{2,1,0:T(8,128)} %get-tuple-element.60), calls=%async_computation.2 | async-start | bytes 393216 | tf_op jit(solution)/shard_map/all_to_all | solution.py:440
  (31 other events, 290.1 us)
